TPU v7x, 128 devices: a whole 4x4x4 slice. The times are simulated.
128 devices in a mesh: ctx: 32 (over x, y, core), head: 4 (over z).
Axes of the slice: x: 4, y: 4, z: 4, core: 2. Of those that a mesh axis runs over, the one named last changes fastest.
Arguments:
- activations: bfloat16 [8192, 2048], P('ctx'), may hold values from -6 to 6
- w_q: bfloat16 [2048, 2048], P(None, 'head'), may hold values from -0.125 to 0.125
- w_k: bfloat16 [2048, 2048], P(None, 'head'), may hold values from -0.125 to 0.125
- w_v: bfloat16 [2048, 4096], P(None, 'head'), may hold values from -0.125 to 0.125
- w_z: bfloat16 [2048, 4096], P(None, 'head'), may hold values from -0.125 to 0.125
- w_a: bfloat16 [2048, 32], P(None, 'head'), may hold values from -0.125 to 0.125
- w_b: bfloat16 [2048, 32], P(None, 'head'), may hold values from -0.125 to 0.125
- conv_q: float32 [4, 2048], P(None, 'head'), may hold values from -3 to 3
- conv_k: float32 [4, 2048], P(None, 'head'), may hold values from -3 to 3
- conv_v: float32 [4, 4096], P(None, 'head'), may hold values from -3 to 3
- a_log: float32 [32], P('head'), may hold values from -9 to -3
- dt_bias: float32 [32], P('head'), may hold values from -1 to 1
- norm_gain: float32 [128], replicated, may hold values from 0.1 to 1.9
- w_o: bfloat16 [4096, 2048], P('head'), may hold values from -0.09375 to 0.09375
Outputs:
- mixed: bfloat16 [8192, 2048], P(('ctx', 'head'))
All inputs are finite; a program needn't handle non-finite values.
Results may differ from a plain program's by a relative error of at most 0.014.
Values may be sent and summed in bfloat16 or wider, within the bound.
A program may use at most 192 MiB of HBM per device.

v0:
```python
import math

import jax
import jax.numpy as jnp
from jax import lax
from jax.sharding import PartitionSpec as P

DK = 128
DV = 128
KERNEL = 4
SPAN = 64


highest = lax.Precision.HIGHEST


def shifted(value, axis, by):
    devices = lax.axis_size(axis)
    pairs = [(i, i + by) for i in range(devices) if 0 <= i + by < devices]
    return lax.ppermute(value, axis, pairs)


def entering(value, axis, join, neutral):
    count, mine = (lax.axis_size(axis), lax.axis_index(axis))
    pieces = jax.tree.map(lambda part: lax.all_gather(part, axis), value)
    subtotal = jax.tree.map(
        lambda part, zero: jnp.full_like(part, 0) + jnp.asarray(zero, part.dtype), value, neutral
    )

    def turn(position, subtotal):
        longer = join(subtotal, jax.tree.map(lambda part: part[position], pieces))
        return jax.tree.map(lambda new, old: jnp.where(position < mine, new, old), longer, subtotal)

    return lax.fori_loop(0, count - 1, turn, subtotal)


def causal_conv(raw, before, taps):
    padded = jnp.concatenate([before.astype(jnp.float32), raw.astype(jnp.float32)], 0)
    width = taps.shape[0]
    total = jnp.zeros(raw.shape, jnp.float32)
    for shift_pos in range(width):
        total = total + taps[shift_pos] * padded[shift_pos : shift_pos + raw.shape[0]]
    return jax.nn.silu(total)


def unit_heads(feature, groups):
    shaped = feature.reshape(feature.shape[0], groups, -1)
    shaped = shaped / jnp.sqrt(jnp.sum(shaped * shaped, -1, keepdims=True) + 1e-06)
    return shaped.reshape(feature.shape)


def block_parts(query, key, value, beta, logdecay):
    extent = query.shape[-2]
    cumulative = jnp.cumsum(logdecay, -1)
    places = jnp.arange(extent)
    strict = (places[:, None] > places[None, :]).astype(jnp.float32)
    lower = places[:, None] >= places[None, :]
    spread = cumulative[..., :, None] - cumulative[..., None, :]
    factor = jnp.exp(jnp.where(lower, spread, 0.0)) * lower.astype(jnp.float32)
    keykey = jnp.einsum("...id,...jd->...ij", key, key, precision=highest)
    system = jnp.eye(extent, dtype=jnp.float32) + beta[..., :, None] * keykey * factor * strict
    scaled = (jnp.exp(cumulative) * beta)[..., None] * key
    w_part = jax.scipy.linalg.solve_triangular(system, scaled, lower=True, unit_diagonal=True)
    u_part = jax.scipy.linalg.solve_triangular(
        system, beta[..., None] * value, lower=True, unit_diagonal=True
    )
    scores = jnp.einsum("...id,...jd->...ij", query, key, precision=highest) * factor
    inside = jnp.einsum("...ij,...jd->...id", scores, u_part, precision=highest)
    effective = jnp.exp(cumulative)[..., None] * query - jnp.einsum(
        "...ij,...jd->...id", scores, w_part, precision=highest
    )
    final = cumulative[..., -1:]
    carried = jnp.exp(final - cumulative)[..., None] * key
    eye_k = jnp.eye(key.shape[-1], dtype=jnp.float32)
    transition = jnp.exp(final)[..., None] * eye_k - jnp.einsum(
        "...id,...ie->...de", carried, w_part, precision=highest
    )
    feed = jnp.einsum("...id,...ie->...de", carried, u_part, precision=highest)
    return (inside, effective, transition, feed)


def by_heads(array, heads, blocks):
    return jnp.transpose(array.reshape(blocks, SPAN, heads, -1), (2, 0, 1, 3))


def compose(earlier, later):
    transit_new = jnp.einsum("hde,hef->hdf", later[0], earlier[0], precision=highest)
    feed_new = jnp.einsum("hde,hef->hdf", later[0], earlier[1], precision=highest) + later[1]
    return (transit_new, feed_new)


def local(
    activations,
    w_q,
    w_k,
    w_v,
    w_z,
    w_a,
    w_b,
    conv_q,
    conv_k,
    conv_v,
    a_log,
    dt_bias,
    norm_gain,
    w_o,
):
    length = activations.shape[0]
    heads = a_log.shape[0]
    key_heads = w_q.shape[1] // DK
    ratio = heads // key_heads
    blocks = length // SPAN
    widths = (w_q.shape[1], w_k.shape[1], w_v.shape[1])
    raw_query = jnp.dot(activations, w_q, preferred_element_type=jnp.float32).astype(jnp.bfloat16)
    raw_key = jnp.dot(activations, w_k, preferred_element_type=jnp.float32).astype(jnp.bfloat16)
    raw_value = jnp.dot(activations, w_v, preferred_element_type=jnp.float32).astype(jnp.bfloat16)
    tail_rows = KERNEL - 1
    joined = jnp.concatenate(
        [
            raw_query[length - tail_rows :],
            raw_key[length - tail_rows :],
            raw_value[length - tail_rows :],
        ],
        1,
    )
    before = shifted(joined, "ctx", 1)
    query = unit_heads(
        causal_conv(raw_query, before[:, : widths[0]], conv_q), key_heads
    ) / math.sqrt(DK)
    key = unit_heads(
        causal_conv(raw_key, before[:, widths[0] : widths[0] + widths[1]], conv_k), key_heads
    )
    value = causal_conv(raw_value, before[:, widths[0] + widths[1] :], conv_v)
    beta = jax.nn.sigmoid(jnp.dot(activations, w_b, preferred_element_type=jnp.float32))
    rate = jnp.exp(a_log) * jax.nn.softplus(
        jnp.dot(activations, w_a, preferred_element_type=jnp.float32) + dt_bias
    )
    q_heads = by_heads(
        jnp.repeat(query.reshape(length, key_heads, DK), ratio, axis=1), heads, blocks
    )
    k_heads = by_heads(jnp.repeat(key.reshape(length, key_heads, DK), ratio, axis=1), heads, blocks)
    v_heads = by_heads(value.reshape(length, heads, DV), heads, blocks)
    b_heads = jnp.transpose(beta).reshape(heads, blocks, SPAN)
    g_heads = -jnp.transpose(rate).reshape(heads, blocks, SPAN)
    inside, effective, transition, feed = block_parts(q_heads, k_heads, v_heads, b_heads, g_heads)
    eye_b = jnp.broadcast_to(jnp.eye(DK, dtype=jnp.float32), (heads, DK, DK))

    def advance(carry, pieces):
        state, product = carry
        inside_c, effect_c, transit_c, feed_c = pieces
        result = inside_c + jnp.einsum("hid,hde->hie", effect_c, state, precision=highest)
        pulled = jnp.einsum("hid,hde->hie", effect_c, product, precision=highest)
        state = jnp.einsum("hde,hef->hdf", transit_c, state, precision=highest) + feed_c
        product = jnp.einsum("hde,hef->hdf", transit_c, product, precision=highest)
        return ((state, product), (result, pulled))

    pieces = tuple((jnp.moveaxis(item, 1, 0) for item in (inside, effective, transition, feed)))
    start_state = jnp.zeros((heads, DK, DV), jnp.float32)
    (local_feed, local_transit), (partial_value, pulls) = lax.scan(
        advance, (start_state, eye_b), pieces
    )
    prefix = entering(
        (local_transit, local_feed),
        "ctx",
        compose,
        (eye_b, jnp.zeros((heads, DK, DV), jnp.float32)),
    )
    incoming = prefix[1]
    core = partial_value + jnp.einsum("nhid,hde->nhie", pulls, incoming, precision=highest)
    core = jnp.transpose(core, (0, 2, 1, 3)).reshape(length, heads, DV)
    gate = jnp.dot(activations, w_z, preferred_element_type=jnp.float32).reshape(length, heads, DV)
    normed = core / jnp.sqrt(jnp.mean(core * core, -1, keepdims=True) + 1e-06)
    gated = (
        (normed * norm_gain * jax.nn.silu(gate)).reshape(length, heads * DV).astype(jnp.bfloat16)
    )
    total = lax.psum_scatter(
        jnp.dot(gated, w_o, preferred_element_type=jnp.float32),
        "head",
        scatter_dimension=0,
        tiled=True,
    )
    return total.astype(jnp.bfloat16)


def solution(mesh):
    in_specs = (
        P("ctx", None),
        P(None, "head"),
        P(None, "head"),
        P(None, "head"),
        P(None, "head"),
        P(None, "head"),
        P(None, "head"),
        P(None, "head"),
        P(None, "head"),
        P(None, "head"),
        P("head"),
        P("head"),
        P(),
        P("head", None),
    )
    out_specs = P(("ctx", "head"), None)
    return jax.shard_map(local, mesh=mesh, in_specs=in_specs, out_specs=out_specs, check_vma=False)
```

profile of v0, /device:TPU:6, one launch (start us, length us, event | category | flops | bytes accessed | tf_op | source)
XLA Modules:
  0.0 503.6 jit_solution(9173836100563061278)
XLA Ops:
  6.5 4.9 fusion.103
  13.8 2.1 collective-permute-start
  18.4 2.7 collective-permute-done
  23.6 2.9 fusion.40
  26.5 158.1 %custom-call.6 = f32[8,4,1,64,64]{3,4,2,1,0:T(8,128)S(1)} custom-call(f32[8,4,1,64,64]{4,3,2,1,0:T(8,128)} %fusion.40), custom_call_target="InvertDiagBlocksLowerTriangular" | custom-call | tf_op jit(solution)/shard_map/jit(_solve_triangular)/vmap(vmap())/triangular_solve | solution.py:63
  186.7 1.8 convolution_multiply_fusion
  189.4 2.1 fusion.57
  191.5 2.1 fusion.55
  193.6 2.2 convolution_bitcast_fusion.3
  195.8 5.3 %convolution_bitcast_fusion.1 = f32[4,8,128,128]{3,2,0,1:T(8,128)} fusion(f32[8,4,64,128]{3,2,1,0:T(8,128)S(1)} %fusion.55, f32[8,4,64,128]{3,2,1,0:T(8,128)S(1)} %bitcast.191, f32[8,4,64]{2,1,0:T(4,128)S(1)} %copy.59), kind=kOutput, calls=%fused_computation.37 | convolution fusion | flops 402915328 | bytes 4202496 | tf_op jit(solution)/shard_map/...id,...ie->...de/dot_general | solution.py:78
  201.2 2.3 fusion.32
  203.5 4.0 bitcast_subtract_fusion
  207.5 35.7 %while.31 = (s32[]{:T(128)}, f32[8,128,128]{2,1,0:T(8,128)}, f32[8,128,128]{2,1,0:T(8,128)S(1)}, f32[4,8,64,128]{3,2,0,1:T(8,128)}, f32[4,8,64,128]{3,2,0,1:T(8,...) while((s32[]{:T(128)}, f32[8,128,128]{2,1,0:T(8,128)}, ...), condition=%wide.region_4.6_spmd.clone, body=%wide.region_3.5_spmd.clone.sunk | while | flops 604438528 | bytes 8129660 | solution.py:159
  208.6 2.3 fusion.157
  210.9 2.5 convolution_add_fusion.5
  213.4 2.3 fusion.158
  217.5 2.3 fusion.157
  219.8 2.5 convolution_add_fusion.5
  222.4 2.3 fusion.158
  226.4 2.3 fusion.157
  228.7 2.5 convolution_add_fusion.5
  231.3 2.3 fusion.158
  235.3 2.3 fusion.157
  237.6 2.5 convolution_add_fusion.5
  240.2 2.3 fusion.158
  244.8 72.3 %all-gather.5.cloned.1.call-done = f32[256,128,128]{2,1,0:T(8,128)} async-done(((f32[8,128,128]{2,1,0:T(8,128)}), f32[256,128,128]{2,1,0:T(8,128)}) %all-gather.5.cloned.1.call-update) | async-done | bytes 16777232 | tf_op jit(solution)/shard_map/all_gather | solution.py:25
  317.2 74.2 %all-gather.7.cloned.1.call-done = f32[256,128,128]{2,1,0:T(8,128)} async-done(((f32[8,128,128]{2,1,0:T(8,128)}), f32[256,128,128]{2,1,0:T(8,128)}) %all-gather.7.cloned.1.call-update) | async-done | bytes 16777232 | tf_op jit(solution)/shard_map/all_gather | solution.py:25
  391.3 60.5 %while.32 = (s32[]{:T(128)}, f32[8,128,128]{2,1,0:T(8,128)S(1)}, s32[]{:T(128)}, f32[32,8,128,128]{3,2,1,0:T(8,128)}, f32[32,8,128,128]{3,2,1,0:T(8,128)}, /*index=5*/s32[]{:T(128)}, s32[]{:T(128)}) while((s32[]{:T(128)}, f32[8,128,128]{2,1,0:T(8,128)S(1)}, s32[]{:T(128)}, f32[32,8,128,128]{3,2,1,0:T(8,128)}, ...), condition=%wide.region_6.8_spmd.clone, body=%wide.region_5.7_spmd.clone.sunk | while | flops 201850880 | bytes 3672671 | solution.py:34
  391.4 2.0 fusion.161
  393.4 1.9 fusion.161
  395.4 1.9 fusion.161
  397.3 1.9 fusion.161
  399.3 1.9 fusion.161
  401.2 1.9 fusion.161
  403.2 1.9 fusion.161
  405.1 1.9 fusion.161
  407.1 1.9 fusion.161
  409.0 1.9 fusion.161
  411.0 1.9 fusion.161
  412.9 1.9 fusion.161
  414.8 1.9 fusion.161
  416.8 1.9 fusion.161
  418.7 1.9 fusion.161
  420.7 1.9 fusion.161
  422.6 1.9 fusion.161
  424.6 1.9 fusion.161
  426.5 1.9 fusion.161
  428.5 1.9 fusion.161
  430.4 1.9 fusion.161
  432.4 1.9 fusion.161
  434.3 1.9 fusion.161
  436.3 1.9 fusion.161
  438.2 1.9 fusion.161
  440.2 1.9 fusion.161
  442.1 1.9 fusion.161
  444.1 1.9 fusion.161
  446.0 1.9 fusion.161
  448.0 1.9 fusion.161
  449.9 1.9 fusion.161
  451.8 2.4 multiply_reduce_fusion
  454.4 1.6 copy.77
  457.3 8.3 %fusion.77 = f32[256,2048]{1,0:T(8,128)} fusion(bf16[1024,2048]{1,0:T(8,128)(2,1)} %param.33, f32[32,8,8,128]{3,2,1,0:T(8,128)} %bitcast.197, f32[32,8,8,128]{3,2,1,0:T(8,128)} %bitcast.198, f32[1024]{0:T(1024)S(1)} %broadcast_bitcast_fusion, bf16[256,2048]{1,0:T(8,128)(2,1)S(1)} %copy-done.4, bf16[2048,1024]{1,0:T(8,128)(2,1)} %param.24), kind=kOutput, calls=%fused_computation.105 | convolution fusion | flops 2149580800 | bytes 13635584 | tf_op jit(solution)/shard_map/dot_general | solution.py:177
  465.7 29.6 %reduce-scatter.2.cloned.1.call-done = f32[64,2048]{1,0:T(8,128)} async-done(((f32[256,2048]{1,0:T(8,128)}), f32[64,2048]{1,0:T(8,128)}) %reduce-scatter.2.cloned.1.call-update) | async-done | bytes 524304 | tf_op jit(solution)/shard_map/reduce_scatter | solution.py:176
  495.3 1.8 convert_element_type.78
  (137 shorter events, 21.2 us)
Async XLA Ops:
  6.5 4.9 copy-start
  6.5 4.9 copy-start.3
  6.5 310.6 %all-gather.5.cloned.1.call-start = ((), (), s32[]{:S(2)}) async-start(), calls=%async_computation.2 | async-start | bytes 17301504 | tf_op jit(solution)/shard_map/all_gather | solution.py:25
  11.4 1.6 copy-start.6
  13.0 2.9 copy-start.12
  13.0 3.0 copy-start.13
  13.0 3.0 copy-start.16
  13.0 3.0 copy-start.9
  13.0 3.0 copy-start.14
  13.0 3.5 copy-start.10
  13.8 4.4 copy-start.11
  13.8 7.3 %copy-start.5 = (f32[256,512]{1,0:T(8,128)S(1)}, f32[256,512]{1,0:T(8,128)}, u32[]{:S(2)}) copy-start(f32[256,512]{1,0:T(8,128)} %get-tuple-element.283) | copy-start | bytes 1572868
  13.8 7.3 %collective-permute-start = (bf16[3,2048]{1,0:T(4,128)(2,1)S(1)}, bf16[3,2048]{1,0:T(4,128)(2,1)S(1)}, u32[]{:S(2)}, u32[]{:S(2)}) collective-permute-start(bf16[3,2048]{1,0:T(4,128)(2,1)S(1)} %pad_maximum_fusion.3), channel_id=1, source_target_pairs={{0,4},{4,8},{8,12},{12,16},{16,20},{20,24},{24,28},{28,32},{32,36}... | collective-permute-start | bytes 36872 | tf_op jit(solution)/shard_map/ppermute | solution.py:20
  186.6 1.9 copy-start.8
  207.5 37.3 %copy-start.15 = (f32[128]{0:T(128)S(1)}, f32[128]{0:T(128)}, u32[]{:S(2)}) copy-start(f32[128]{0:T(128)} %param.32) | copy-start | bytes 1540
  243.2 0.8 copy-start.2
  244.0 147.4 %all-gather.7.cloned.1.call-start = ((), (), s32[]{:S(2)}) async-start(), calls=%async_computation.3 | async-start | bytes 17301504 | tf_op jit(solution)/shard_map/all_gather | solution.py:25
  244.7 250.6 %reduce-scatter.2.cloned.1.call-start = ((), (), s32[]{:S(2)}) async-start(), calls=%async_computation.1 | async-start | bytes 2621440 | tf_op jit(solution)/shard_map/reduce_scatter | solution.py:176
  391.3 60.5 %copy-start.7 = (f32[4,8,64,128]{3,2,0,1:T(8,128)S(1)}, f32[4,8,64,128]{3,2,0,1:T(8,128)}, u32[]{:S(2)}) copy-start(f32[4,8,64,128]{3,2,0,1:T(8,128)} %get-tuple-element.150) | copy-start | bytes 3145732
  454.3 3.0 copy-start.4
  457.3 39.7 %copy-start.1 = (bf16[2048,512]{1,0:T(8,128)(2,1)S(1)}, bf16[2048,512]{1,0:T(8,128)(2,1)}, u32[]{:S(2)}) copy-start(bf16[2048,512]{1,0:T(8,128)(2,1)} %param.21) | copy-start | bytes 6291460
Sparse Core Ops, SparseCore 0:
  244.1 73.0 all-gather.4
  319.4 71.8 all-gather.6
  465.8 29.4 reduce-scatter.1
where the time goes:
time: 506 us; the launch traced here: 504 us
  waiting for transfers between devices  180 us (36%)
  other arithmetic  164 us (32%)
  matrix products  131 us (26%)
  between operations  13.6 us (3%)
  local copies, waits for them, and re-layouts  11.9 us (2%)
    another operation x4, other arithmetic, block_parts(): jax.scipy.linalg.solve_triangular(system, scaled, lower=True, unit_diagon...  158 us
    all_gather x2, waiting for transfers between devices, entering(): pieces = jax.tree.map(lambda part: lax.all_gather(part, axis), value)  147 us
    dot_general x31, matrix products, compose(): jnp.einsum('hde,hef->hdf', later[0], earlier[1], precision=highest)  58.2 us
    reduce_scatter x1, waiting for transfers between devices, local(): lax.psum_scatter(jnp.dot(gated, w_o, preferred_element_type=jnp.float32),...  29.6 us
  transfers between devices with their start and end apart: 4, of which 4 were waited for; matrix products, arithmetic and copies ran while one was open for 0% of the time, Pallas kernels for 0%

commit v1 on v0

v1 whole, which is shorter than its diff:
```python
import functools
import math

import jax
import jax.numpy as jnp
from jax import lax
from jax.experimental import pallas as pl
from jax.experimental.pallas import tpu as pltpu
from jax.sharding import PartitionSpec as P

DK = 128
DV = 128
KERNEL = 4
HALO = 8
GROUP = 8
MESH = pl.DeviceIdType.MESH
F32 = jnp.float32
BF16 = jnp.bfloat16
VMEM_LIMIT = 56 * 1024 * 1024


def dot(a, b, dims=((1,), (0,))):
    return lax.dot_general(a, b, (dims, ((), ())), preferred_element_type=F32)


NT = ((1,), (1,))
TN = ((0,), (0,))


def conv_silu(pad, taps, rows):
    total = taps[KERNEL - 1 : KERNEL] * pad[HALO : HALO + rows]
    for back in range(1, KERNEL):
        at = HALO - back
        total = total + taps[KERNEL - 1 - back : KERNEL - back] * pad[at : at + rows]
    return total / (1.0 + jnp.exp(-total))


def unit(feature, scale):
    norm = jnp.sum(feature * feature, -1, keepdims=True) + 1e-06
    return feature * (lax.rsqrt(norm) * scale)


def invert(blocks, differ):
    one = jnp.where(differ == 0, 1.0, 0.0).astype(BF16)
    size = blocks[0].shape[0]
    inverses = None
    width = 1
    while width < size:
        mask = jnp.where((differ >= width) & (differ < 2 * width), 1.0, 0.0).astype(BF16)
        lows = [block * mask for block in blocks]
        if inverses is None:
            inverses = [one - low for low in lows]
        else:
            right = [dot(low, inv).astype(BF16) for low, inv in zip(lows, inverses)]
            left = [dot(inv, r).astype(BF16) for inv, r in zip(inverses, right)]
            inverses = [inv - l for inv, l in zip(inverses, left)]
        width *= 2
    return inverses


def gdn_kernel(
    rq, rk, rv, hq, hk, hv, cq, ck, cv, beta_ref, cum_ref, cumt_ref, m_out, inside_out, eff_out, pad
):
    rows = rq.shape[0]
    half = rows // 2
    key_heads = rq.shape[1] // DK
    ratio = rv.shape[1] // rq.shape[1]

    def smooth(raw, halo, taps, at):
        pad[0:HALO] = halo[:, at : at + DK].astype(F32)
        pad[HALO:] = raw[:, at : at + DK].astype(F32)
        return conv_silu(pad, taps[:, at : at + DK], rows)

    row_at = lax.broadcasted_iota(jnp.int32, (half, half), 0)
    col_at = lax.broadcasted_iota(jnp.int32, (half, half), 1)
    differ = row_at ^ col_at
    lower = row_at >= col_at
    strict = row_at > col_at
    heads = []
    for h in range(key_heads):
        query = unit(smooth(rq, hq, cq, h * DK), 1.0 / math.sqrt(DK))
        key = unit(smooth(rk, hk, ck, h * DK), 1.0)
        qb, kb = query.astype(BF16), key.astype(BF16)
        kk11 = dot(kb[:half], kb[:half], NT)
        kk22 = dot(kb[half:], kb[half:], NT)
        kk21 = dot(kb[half:], kb[:half], NT)
        qk11 = dot(qb[:half], kb[:half], NT)
        qk22 = dot(qb[half:], kb[half:], NT)
        qk21 = dot(qb[half:], kb[:half], NT)
        for r in range(ratio):
            j = h * ratio + r
            value = smooth(rv, hv, cv, j * DV)
            beta = beta_ref[0, :, j : j + 1]
            cum = cum_ref[0, :, j : j + 1]
            cum_row = cumt_ref[0, j : j + 1, :]
            f11 = jnp.exp(jnp.where(lower, cum[:half] - cum_row[:, :half], -1e30))
            f22 = jnp.exp(jnp.where(lower, cum[half:] - cum_row[:, half:], -1e30))
            f21 = jnp.exp(cum[half:] - cum_row[:, :half])
            a11 = jnp.where(strict, beta[:half] * kk11 * f11, 0.0).astype(BF16)
            a22 = jnp.where(strict, beta[half:] * kk22 * f22, 0.0).astype(BF16)
            a21 = (beta[half:] * kk21 * f21).astype(BF16)
            s11 = (qk11 * f11).astype(BF16)
            s22 = (qk22 * f22).astype(BF16)
            s21 = (qk21 * f21).astype(BF16)
            grow = jnp.exp(cum)
            rhs = jnp.concatenate([key * (grow * beta), value * beta], 1)
            heads.append((j, query, kb, cum, grow, a11, a22, a21, s11, s22, s21, rhs))
    inverses = invert([a for item in heads for a in (item[5], item[6])], differ)
    eye = jnp.where(
        lax.broadcasted_iota(jnp.int32, (DK, DK), 0) == lax.broadcasted_iota(jnp.int32, (DK, DK), 1), 1.0, 0.0
    )
    for n, (j, query, kb, cum, grow, _, _, a21, s11, s22, s21, rhs) in enumerate(heads):
        wu1 = dot(inverses[2 * n], rhs[:half].astype(BF16)).astype(BF16)
        low = rhs[half:] - dot(a21, wu1)
        wu2f = dot(inverses[2 * n + 1], low.astype(BF16))
        wu2 = wu2f.astype(BF16)
        in1 = dot(s11, wu1)
        in2 = dot(s21, wu1) + dot(s22, wu2)
        inside_out[0:half, j * DV : (j + 1) * DV] = in1[:, DK:]
        inside_out[half:, j * DV : (j + 1) * DV] = in2[:, DK:]
        eff = grow * query
        eff_out[0:half, j * DK : (j + 1) * DK] = (eff[:half] - in1[:, :DK]).astype(BF16)
        eff_out[half:, j * DK : (j + 1) * DK] = (eff[half:] - in2[:, :DK]).astype(BF16)
        final = cum[rows - 1 : rows]
        carry = jnp.exp(final - cum)
        tf = dot(kb[:half], (wu1.astype(F32) * carry[:half]).astype(BF16), TN) + dot(
            kb[half:], (wu2f * carry[half:]).astype(BF16), TN
        )
        m_out[j, :, :DK] = ((jnp.exp(final) - 1.0) * eye - tf[:, :DK]).astype(BF16)
        m_out[j, :, DK:] = tf[:, DK:].astype(BF16)


def gdn(raw_q, raw_k, raw_v, halo, conv_q, conv_k, conv_v, beta, cum, steps):
    rows = raw_q.shape[0]
    heads = beta.shape[1]
    per = heads // steps
    kw, vw = raw_q.shape[1] // steps, raw_v.shape[1] // steps
    w = raw_q.shape[1]

    def cols(n, width, first=0):
        return pl.BlockSpec((n, width), lambda s: (0, s + first))

    beta3 = jnp.transpose(beta.reshape(rows, steps, per), (1, 0, 2))
    cum3 = jnp.transpose(cum.reshape(rows, steps, per), (1, 0, 2))
    cumt = jnp.transpose(cum).reshape(steps, per, rows)
    three = lambda s: (s, 0, 0)
    return pl.pallas_call(
        gdn_kernel,
        grid=(steps,),
        in_specs=[
            cols(rows, kw),
            cols(rows, kw),
            cols(rows, vw),
            cols(HALO, kw),
            cols(HALO, kw, w // kw),
            cols(HALO, vw, 2 * w // vw),
            cols(KERNEL, kw),
            cols(KERNEL, kw),
            cols(KERNEL, vw),
            pl.BlockSpec((1, rows, per), three),
            pl.BlockSpec((1, rows, per), three),
            pl.BlockSpec((1, per, rows), three),
        ],
        out_specs=[
            pl.BlockSpec((per, DK, DK + DV), three),
            cols(rows, vw),
            cols(rows, per * DK),
        ],
        out_shape=[
            jax.ShapeDtypeStruct((heads, DK, DK + DV), BF16),
            jax.ShapeDtypeStruct((rows, heads * DV), F32),
            jax.ShapeDtypeStruct((rows, heads * DK), BF16),
        ],
        scratch_shapes=[pltpu.VMEM((HALO + rows, DK), F32)],
        compiler_params=pltpu.CompilerParams(vmem_limit_bytes=VMEM_LIMIT),
        name="gdn_local",
    )(raw_q, raw_k, raw_v, halo, halo, halo, conv_q, conv_k, conv_v, beta3, cum3, cumt)


def remote(src, dst, send, recv, ctx, head):
    return pltpu.make_async_remote_copy(
        src_ref=src, dst_ref=dst, send_sem=send, recv_sem=recv, device_id=(ctx, head), device_id_type=MESH
    )


def compose(later, earlier):
    return later + earlier + dot(later[:, :DK].astype(BF16), earlier.astype(BF16))


def exchange_kernel(groups, m_ref, s_out, land, total, land2, pref, state, sbuf, send1, recv1, send2, recv2, send3, recv3):
    c = lax.axis_index("ctx")
    z = lax.axis_index("head")
    g = c // GROUP
    me = lax.rem(c, GROUP)
    base = g * GROUP

    barrier = pltpu.get_barrier_semaphore()
    for d in range(1, GROUP):
        peer = base + lax.rem(me + d, GROUP)
        pl.semaphore_signal(barrier, inc=1, device_id=(peer, z), device_id_type=MESH)
    for d in range(1, groups):
        peer = lax.rem(g + d, groups) * GROUP + me
        pl.semaphore_signal(barrier, inc=1, device_id=(peer, z), device_id_type=MESH)
    pl.semaphore_wait(barrier, GROUP - 1 + groups - 1)

    for d in range(1, GROUP):
        peer = lax.rem(me + d, GROUP)
        remote(m_ref.at[peer], land.at[me], send1.at[d], recv1.at[me], base + peer, z).start()
    land[me] = m_ref[me]
    for d in range(1, GROUP):
        peer = lax.rem(me + d, GROUP)
        remote(m_ref.at[peer], land.at[peer], send1.at[d], recv1.at[peer], base + peer, z).wait_recv()

    maps = [land[j].astype(F32) for j in range(GROUP)]
    p01 = compose(maps[1], maps[0])
    p23 = compose(maps[3], maps[2])
    p45 = compose(maps[5], maps[4])
    p67 = compose(maps[7], maps[6])
    p03 = compose(p23, p01)
    p47 = compose(p67, p45)
    whole = compose(p47, p03)
    total[...] = whole.astype(BF16)
    for other in range(1, groups):

        @pl.when(g < other)
        def _():
            remote(total, land2.at[g], send2.at[other], recv2.at[g], other * GROUP + me, z).start()

    p02 = compose(maps[2], p01)
    p04 = compose(maps[4], p03)
    p05 = compose(p45, p03)
    p06 = compose(maps[6], p05)
    for j, item in enumerate((maps[0], p01, p02, p03, p04, p05, p06)):
        pref[j] = item

    state[...] = jnp.zeros_like(state)
    for other in range(groups - 1):

        @pl.when(other < g)
        def _():
            remote(total, land2.at[other], send2.at[0], recv2.at[other], other * GROUP + me, z).wait_recv()
            now = state[...]
            step = land2[other]
            state[...] = now + step[:, DK:].astype(F32) + dot(step[:, :DK], now.astype(BF16))

    now = state[...]
    low = now.astype(BF16)
    for j in range(GROUP):
        if j == 0:
            sbuf[j] = low
        else:
            item = pref[j - 1]
            sbuf[j] = (now + item[:, DK:] + dot(item[:, :DK].astype(BF16), low)).astype(BF16)

        @pl.when(j != me)
        def _(j=j):
            remote(sbuf.at[j], s_out.at[me], send3.at[j], recv3.at[me], base + j, z).start()

    s_out[me] = sbuf[me]
    for j in range(GROUP):

        @pl.when(j != me)
        def _(j=j):
            remote(sbuf.at[j], s_out.at[j], send3.at[j], recv3.at[j], base + j, z).wait_recv()

    for d in range(1, GROUP):
        peer = lax.rem(me + d, GROUP)
        remote(m_ref.at[peer], land.at[me], send1.at[d], recv1.at[me], base + peer, z).wait_send()
    for other in range(1, groups):

        @pl.when(g < other)
        def _():
            remote(total, land2.at[g], send2.at[other], recv2.at[g], other * GROUP + me, z).wait_send()

    for j in range(GROUP):

        @pl.when(j != me)
        def _(j=j):
            remote(sbuf.at[j], s_out.at[me], send3.at[j], recv3.at[me], base + j, z).wait_send()


def exchange(maps, groups):
    heads = maps.shape[0]
    vmem = pl.BlockSpec(memory_space=pltpu.VMEM)
    return pl.pallas_call(
        functools.partial(exchange_kernel, groups),
        in_specs=[vmem],
        out_specs=vmem,
        out_shape=jax.ShapeDtypeStruct((heads, DK, DV), BF16),
        scratch_shapes=[
            pltpu.VMEM((GROUP, DK, DK + DV), BF16),
            pltpu.VMEM((DK, DK + DV), BF16),
            pltpu.VMEM((groups, DK, DK + DV), BF16),
            pltpu.VMEM((GROUP, DK, DK + DV), F32),
            pltpu.VMEM((DK, DV), F32),
            pltpu.VMEM((GROUP, DK, DV), BF16),
            pltpu.SemaphoreType.DMA((GROUP,)),
            pltpu.SemaphoreType.DMA((GROUP,)),
            pltpu.SemaphoreType.DMA((groups,)),
            pltpu.SemaphoreType.DMA((groups,)),
            pltpu.SemaphoreType.DMA((GROUP,)),
            pltpu.SemaphoreType.DMA((GROUP,)),
        ],
        compiler_params=pltpu.CompilerParams(
            collective_id=0, has_side_effects=True, vmem_limit_bytes=VMEM_LIMIT
        ),
        name="states",
    )(maps)


def finish_kernel(inside, eff, s_in, gate, gain, w_o, part, gated):
    heads = s_in.shape[0]
    for j in range(heads):
        at = slice(j * DV, (j + 1) * DV)
        core = inside[:, at] + dot(eff[:, at], s_in[j])
        scale = lax.rsqrt(jnp.mean(core * core, -1, keepdims=True) + 1e-06)
        z = gate[:, at]
        gated[:, at] = (core * scale * gain[...] * (z / (1.0 + jnp.exp(-z)))).astype(BF16)
    width = 512
    for n in range(part.shape[2] // width):
        at = slice(n * width, (n + 1) * width)
        out = dot(gated[...], w_o[:, at]).astype(BF16)
        part[:, :, at] = out.reshape(part.shape[0], part.shape[1], width)


def finish(inside, eff, s_in, gate, gain, w_o, parts):
    rows = inside.shape[0]
    vmem = pl.BlockSpec(memory_space=pltpu.VMEM)
    return pl.pallas_call(
        finish_kernel,
        in_specs=[vmem] * 6,
        out_specs=vmem,
        out_shape=jax.ShapeDtypeStruct((parts, rows // parts, w_o.shape[1]), BF16),
        scratch_shapes=[pltpu.VMEM(inside.shape, BF16)],
        compiler_params=pltpu.CompilerParams(vmem_limit_bytes=VMEM_LIMIT),
        name="gate_and_project",
    )(inside, eff, s_in, gate, gain.reshape(1, -1), w_o)


def scatter_kernel(part, out, relay, sums, land, rsend, rrecv, dsend, drecv):
    c = lax.axis_index("ctx")
    z = lax.axis_index("head")
    up, down, far = lax.rem(z + 1, 4), lax.rem(z + 3, 4), lax.rem(z + 2, 4)
    width = part.shape[2] // 2
    lo, hi = slice(0, width), slice(width, 2 * width)

    barrier = pltpu.get_barrier_semaphore()
    for peer in (up, down):
        pl.semaphore_signal(barrier, inc=1, device_id=(c, peer), device_id_type=MESH)
    pl.semaphore_wait(barrier, 2)

    relays = (
        remote(part.at[far, :, lo], relay.at[0], rsend.at[0], rrecv.at[0], c, up),
        remote(part.at[far, :, hi], relay.at[1], rsend.at[1], rrecv.at[1], c, down),
    )
    direct = (
        remote(part.at[up, :, hi], land.at[0, :, hi], dsend.at[0], drecv.at[0], c, up),
        remote(part.at[down, :, lo], land.at[1, :, lo], dsend.at[1], drecv.at[1], c, down),
    )
    summed = (
        remote(sums.at[0], land.at[0, :, lo], dsend.at[2], drecv.at[2], c, up),
        remote(sums.at[1], land.at[1, :, hi], dsend.at[3], drecv.at[3], c, down),
    )
    for copy in relays + direct:
        copy.start()
    for k, (peer, half) in enumerate(((up, lo), (down, hi))):
        relays[k].wait_recv()
        sums[k] = (part[peer, :, half].astype(F32) + relay[k].astype(F32)).astype(BF16)
        summed[k].start()
    for copy in direct + summed:
        copy.wait_recv()
    out[...] = (part[z].astype(F32) + land[0].astype(F32) + land[1].astype(F32)).astype(BF16)
    for copy in relays + direct + summed:
        copy.wait_send()


def scatter(part):
    parts, rows, width = part.shape
    vmem = pl.BlockSpec(memory_space=pltpu.VMEM)
    return pl.pallas_call(
        scatter_kernel,
        in_specs=[vmem],
        out_specs=vmem,
        out_shape=jax.ShapeDtypeStruct((rows, width), BF16),
        scratch_shapes=[
            pltpu.VMEM((2, rows, width // 2), BF16),
            pltpu.VMEM((2, rows, width // 2), BF16),
            pltpu.VMEM((2, rows, width), BF16),
            pltpu.SemaphoreType.DMA((2,)),
            pltpu.SemaphoreType.DMA((2,)),
            pltpu.SemaphoreType.DMA((4,)),
            pltpu.SemaphoreType.DMA((4,)),
        ],
        compiler_params=pltpu.CompilerParams(
            collective_id=1, has_side_effects=True, vmem_limit_bytes=VMEM_LIMIT
        ),
        name="sum_over_heads",
    )(part)


def local(
    activations, w_q, w_k, w_v, w_z, w_a, w_b, conv_q, conv_k, conv_v, a_log, dt_bias, norm_gain, w_o
):
    length = activations.shape[0]
    ctx = lax.axis_size("ctx")
    raw_q = jnp.dot(activations, w_q, preferred_element_type=F32).astype(BF16)
    raw_k = jnp.dot(activations, w_k, preferred_element_type=F32).astype(BF16)
    raw_v = jnp.dot(activations, w_v, preferred_element_type=F32).astype(BF16)
    tail = jnp.concatenate([raw[length - HALO :] for raw in (raw_q, raw_k, raw_v)], 1)
    halo = lax.ppermute(tail, "ctx", [(i, i + 1) for i in range(ctx - 1)])
    beta = jax.nn.sigmoid(jnp.dot(activations, w_b, preferred_element_type=F32))
    rate = jnp.exp(a_log) * jax.nn.softplus(
        jnp.dot(activations, w_a, preferred_element_type=F32) + dt_bias
    )
    cum = jnp.cumsum(-rate, 0)
    gate = jnp.dot(activations, w_z, preferred_element_type=F32)
    maps, inside, eff = gdn(raw_q, raw_k, raw_v, halo, conv_q, conv_k, conv_v, beta, cum, 2)
    states = exchange(maps, ctx // GROUP)
    part = finish(inside, eff, states, gate, norm_gain, w_o, lax.axis_size("head"))
    return scatter(part)


def solution(mesh):
    in_specs = (
        P("ctx", None),
        P(None, "head"),
        P(None, "head"),
        P(None, "head"),
        P(None, "head"),
        P(None, "head"),
        P(None, "head"),
        P(None, "head"),
        P(None, "head"),
        P(None, "head"),
        P("head"),
        P("head"),
        P(),
        P("head", None),
    )
    out_specs = P(("ctx", "head"), None)
    return jax.shard_map(local, mesh=mesh, in_specs=in_specs, out_specs=out_specs, check_vma=False)
```

time: 506 us -> 80.9 us (0.16)
  waiting for transfers between devices: 180 us -> 0.01 us
  other arithmetic: 164 us -> 0.78 us
  matrix products: 131 us -> 11.7 us
  Pallas kernels: 0 us -> 58.1 us
  between operations: 13.6 us -> 0.18 us
    another operation x7 -> x4, other arithmetic: 159 us -> 0.77 us  [the longest x4 158 us: block_parts(): jax.scipy.linalg.solve_triangular(system, scaled, lower=True, unit_diagon...]
    all_gather x2 -> x0, waiting for transfers between devices: 147 us -> none  [entering(): pieces = jax.tree.map(lambda part: lax.all_gather(part, axis), value)]
    dot_general x60 -> x6, matrix products: 127 us -> 11.7 us  [the longest x1 4.43 us: local(): gate = jnp.dot(activations, w_z, preferred_element_type=F32)]
    pallas_call x0 -> x4, Pallas kernels: none -> 58.1 us  [the longest x1 24.2 us: exchange(): pl.pallas_call(functools.partial(exchange_kernel, groups), in_specs=[vmem...]
    reduce_scatter x1 -> x0, waiting for transfers between devices: 29.6 us -> none  [local(): lax.psum_scatter(jnp.dot(gated, w_o, preferred_element_type=jnp.float32),...]
    while x39 -> x0, local copies, waits for them, and re-layouts: 5.42 us -> none
  transfers between devices with their start and end apart: 4 -> 1, of which waited for: 4 -> 0; matrix products, arithmetic and copies ran while one was open for 0% -> 11% of each run, Pallas kernels for 0% -> 0%
where the time goes in v1:
time: 80.9 us; the launch traced here: 80.6 us
  Pallas kernels  58.1 us (72%)
  matrix products  11.7 us (14%)
  local copies, waits for them, and re-layouts  7.9 us (10%)
  starting transfers between devices  1.91 us (2%)
    pallas_call x1, Pallas kernels, exchange(): pl.pallas_call(functools.partial(exchange_kernel, groups), in_specs=[vmem...  24.2 us
    pallas_call x1, Pallas kernels, scatter(): pl.pallas_call(scatter_kernel, in_specs=[vmem], out_specs=vmem, out_shape...  15.8 us
    pallas_call x1, Pallas kernels, gdn(): pl.pallas_call(gdn_kernel, grid=(steps,), in_specs=[cols(rows, kw), cols(...  12.3 us
    pallas_call x1, Pallas kernels, finish(): pl.pallas_call(finish_kernel, in_specs=[vmem] * 6, out_specs=vmem, out_sh...  5.81 us
    unnamed x23, local copies, waits for them, and re-layouts  5.37 us
    dot_general x1, matrix products, local(): gate = jnp.dot(activations, w_z, preferred_element_type=F32)  4.43 us
    dot_general x1, matrix products, local(): raw_k = jnp.dot(activations, w_k, preferred_element_type=F32).astype(BF16)  2.7 us
    dot_general x1, matrix products, local(): raw_q = jnp.dot(activations, w_q, preferred_element_type=F32).astype(BF16)  2.47 us
  transfers between devices with their start and end apart: 1, of which 0 were waited for; matrix products, arithmetic and copies ran while one was open for 11% of the time, Pallas kernels for 0%

profile of v1, /device:TPU:6, one launch (start us, length us, event | category | flops | bytes accessed | tf_op | source)
XLA Modules:
  0.0 80.6 jit_solution(17282180477009733069)
XLA Ops:
  0.0 0.0 copy-start
  0.0 0.0 copy-start.1
  0.0 0.0 copy-start.9
  0.0 1.6 %copy-done = bf16[2048,512]{1,0:T(8,128)(2,1)S(1)} copy-done((bf16[2048,512]{1,0:T(8,128)(2,1)S(1)}, bf16[2048,512]{1,0:T(8,128)(2,1)}, u32[]{:S(2)}) %copy-start) | copy-done | bytes 2097176
  1.6 2.5 %convolution_convert_fusion.2.rq = bf16[256,512]{1,0:T(8,128)(2,1)S(1)} fusion(bf16[256,2048]{1,0:T(8,128)(2,1)} %param.14, bf16[2048,512]{1,0:T(8,128)(2,1)S(1)} %copy-done), kind=kOutput, calls=%fused_computation.2 | convolution fusion | flops 537001984 | bytes 3407872 | tf_op jit(solution)/shard_map/dot_general | solution.py:406
  4.1 0.0 copy-start.4
  4.1 2.7 %convolution_convert_fusion.1.rk = bf16[256,512]{1,0:T(8,128)(2,1)S(1)} fusion(bf16[256,2048]{1,0:T(8,128)(2,1)} %param.14, bf16[2048,512]{1,0:T(8,128)(2,1)} %param.16), kind=kOutput, calls=%fused_computation.1 | convolution fusion | flops 537001984 | bytes 3407872 | tf_op jit(solution)/shard_map/dot_general | solution.py:407
  6.8 0.0 copy-start.5
  6.8 0.7 copy-done.5
  7.5 0.0 copy-start.10
  7.5 0.0 copy-start.6
  7.5 0.0 copy-start.8
  7.5 0.0 copy-done.1
  7.5 0.0 copy-done.9
  7.5 0.0 copy-start.7
  7.5 1.3 %convolution_convert_fusion.rv = bf16[256,1024]{1,0:T(8,128)(2,1)S(1)} fusion(bf16[256,2048]{1,0:T(8,128)(2,1)S(1)} %copy-done.1, bf16[2048,1024]{1,0:T(8,128)(2,1)S(1)} %copy-done.9), kind=kOutput, calls=%fused_computation | convolution fusion | flops 1074003968 | bytes 5767168 | tf_op jit(solution)/shard_map/dot_general | solution.py:408
  8.8 0.0 copy-done.4
  8.9 0.0 copy-start.2
  8.9 0.8 copy-done.2
  9.7 1.9 %collective-permute-start = (bf16[8,2048]{1,0:T(8,128)(2,1)S(1)}, bf16[8,2048]{1,0:T(8,128)(2,1)S(1)}, u32[]{:S(2)}, u32[]{:S(2)}) collective-permute-start(bf16[8,2048]{1,0:T(8,128)(2,1)S(1)} %pad_maximum_fusion), channel_id=1, source_target_pairs={{0,4},{4,8},{8,12},{12,16},{16,20},{20,24},{24,28},{28,32},{32,36}... | collective-permute-start | bytes 98312 | tf_op jit(solution)/shard_map/ppermute | solution.py:410
  11.6 0.0 copy-done.10
  11.6 0.0 copy-done.6
  11.6 0.0 copy-done.8
  11.6 0.4 fusion.5
  12.0 0.6 reduce-window.6
  12.6 0.2 slice_reduce_fusion
  12.8 0.1 fusion.19
  12.9 0.0 copy-done.7
  12.9 0.4 fusion.2
  13.3 4.4 %fusion.6.gate = f32[256,1024]{1,0:T(8,128)} fusion(bf16[256,2048]{1,0:T(8,128)(2,1)S(1)} %copy-done.1, bf16[2048,1024]{1,0:T(8,128)(2,1)} %param.18), kind=kOutput, calls=%fused_computation.15 | convolution fusion | flops 1073741824 | bytes 6291456 | tf_op jit(solution)/shard_map/dot_general | solution.py:416
  17.7 0.1 broadcast_add_fusion
  17.8 0.6 reduce_window_sum.21.cumt_ref
  18.4 0.9 %copy.16 = f32[256,2,4]{2,0,1:T(8,128)} copy(f32[256,2,4]{0,2,1:T(4,128)S(1)} %reshape.25) | data formatting | bytes 16384 | tf_op jit(solution)/shard_map/reshape | solution.py:143
  19.3 0.9 %copy.17 = f32[256,2,4]{2,0,1:T(8,128)} copy(f32[256,2,4]{0,2,1:T(4,128)S(1)} %reshape.28) | data formatting | bytes 16384 | tf_op jit(solution)/shard_map/reshape | solution.py:144
  20.1 0.0 collective-permute-done.hq.hk.hv
  20.1 0.0 copy-start.3
  20.1 0.6 copy-done.3
  20.7 12.3 %gdn_local.1 = (bf16[8,128,256]{2,1,0:T(8,128)(2,1)}, f32[256,1024]{1,0:T(8,128)}, bf16[256,1024]{1,0:T(8,128)(2,1)}) custom-call(bf16[256,512]{1,0:T(8,128)(2,1)} %copy-done.4, bf16[256,512]{1,0:T(8,128)(2,1)} %copy-done.5, bf16[256,1024]{1,0:T(8,128)(2,1)} %copy-done.2, bf16[8,2048]{1,0:T(8,128)(2,1)} %copy-done.3, bf16[8,2048]{1,0:T(8,128)(2,1)} %copy-done.3, ...), custom_call_target="tpu_custom_call" | custom-call | tf_op jit(solution)/shard_map/gdn_local/pallas_call | solution.py:147
  33.0 24.2 %states.1.s_in = bf16[8,128,128]{2,1,0:T(8,128)(2,1)} custom-call(bf16[8,128,256]{2,1,0:T(8,128)(2,1)} %get-tuple-element.10.m_ref), custom_call_target="tpu_custom_call" | custom-call | tf_op jit(solution)/shard_map/states/pallas_call | solution.py:285
  57.3 5.8 %gate_and_project.1.part = bf16[4,64,2048]{2,1,0:T(8,128)(2,1)} custom-call(f32[256,1024]{1,0:T(8,128)} %get-tuple-element.8.inside, bf16[256,1024]{1,0:T(8,128)(2,1)} %get-tuple-element.9.eff, bf16[8,128,128]{2,1,0:T(8,128)(2,1)} %states.1.s_in, f32[256,1024]{1,0:T(8,128)} %fusion.6.gate, f32[1,128]{1,0:T(1,128)} %bitcast.27, bf16[1024,2048]{1,0:T(8,128)(2,1)} %w_o.1), custom_call_target="tpu_custom_call" | custom-call | tf_op jit(solution)/shard_map/gate_and_project/pallas_call | solution.py:329
  63.1 15.8 %sum_over_heads.1 = bf16[64,2048]{1,0:T(8,128)(2,1)} custom-call(bf16[4,64,2048]{2,1,0:T(8,128)(2,1)} %gate_and_project.1.part), custom_call_target="tpu_custom_call" | custom-call | tf_op jit(solution)/shard_map/sum_over_heads/pallas_call | solution.py:380
  78.9 1.7 %copy.20 = bf16[64,2048]{1,0:T(8,128)(2,1)} copy(bf16[64,2048]{1,0:T(8,128)(2,1)} %sum_over_heads.1) | data formatting | bytes 524288
  (10 shorter events, 0.1 us)
Async XLA Ops:
  0.0 1.6 %copy-start = (bf16[2048,512]{1,0:T(8,128)(2,1)S(1)}, bf16[2048,512]{1,0:T(8,128)(2,1)}, u32[]{:S(2)}) copy-start(bf16[2048,512]{1,0:T(8,128)(2,1)} %param.15) | copy-start | bytes 6291460
  0.0 7.5 %copy-start.1 = (bf16[256,2048]{1,0:T(8,128)(2,1)S(1)}, bf16[256,2048]{1,0:T(8,128)(2,1)}, u32[]{:S(2)}) copy-start(bf16[256,2048]{1,0:T(8,128)(2,1)} %param.14) | copy-start | bytes 3145732
  0.0 7.5 %copy-start.9 = (bf16[2048,1024]{1,0:T(8,128)(2,1)S(1)}, bf16[2048,1024]{1,0:T(8,128)(2,1)}, u32[]{:S(2)}) copy-start(bf16[2048,1024]{1,0:T(8,128)(2,1)} %param.17) | copy-start | bytes 12582916
  4.1 4.8 %copy-start.4 = (bf16[256,512]{1,0:T(8,128)(2,1)}, bf16[256,512]{1,0:T(8,128)(2,1)S(1)}, u32[]{:S(2)}) copy-start(bf16[256,512]{1,0:T(8,128)(2,1)S(1)} %convolution_convert_fusion.2.rq) | copy-start | bytes 786436
  6.8 0.7 copy-start.5
  7.5 4.1 %copy-start.10 = (f32[8]{0:T(128)S(1)}, f32[8]{0:T(128)}, u32[]{:S(2)}) copy-start(f32[8]{0:T(128)} %param.24) | copy-start | bytes 100
  7.5 4.1 %copy-start.6 = (bf16[2048,8]{0,1:T(8,128)(2,1)S(1)}, bf16[2048,8]{0,1:T(8,128)(2,1)}, u32[]{:S(2)}) copy-start(bf16[2048,8]{0,1:T(8,128)(2,1)} %param.19) | copy-start | bytes 98308
  7.5 4.1 %copy-start.8 = (f32[8]{0:T(128)S(1)}, f32[8]{0:T(128)}, u32[]{:S(2)}) copy-start(f32[8]{0:T(128)} %param.25) | copy-start | bytes 100
  7.5 5.4 %copy-start.7 = (bf16[2048,8]{0,1:T(8,128)(2,1)S(1)}, bf16[2048,8]{0,1:T(8,128)(2,1)}, u32[]{:S(2)}) copy-start(bf16[2048,8]{0,1:T(8,128)(2,1)} %param.20) | copy-start | bytes 98308
  8.9 0.8 copy-start.2
  9.7 10.5 %collective-permute-start = (bf16[8,2048]{1,0:T(8,128)(2,1)S(1)}, bf16[8,2048]{1,0:T(8,128)(2,1)S(1)}, u32[]{:S(2)}, u32[]{:S(2)}) collective-permute-start(bf16[8,2048]{1,0:T(8,128)(2,1)S(1)} %pad_maximum_fusion), channel_id=1, source_target_pairs={{0,4},{4,8},{8,12},{12,16},{16,20},{20,24},{24,28},{28,32},{32,36}... | collective-permute-start | bytes 98312 | tf_op jit(solution)/shard_map/ppermute | solution.py:410
  20.1 0.6 copy-start.3

commit v2 on v0

v2 whole, which is shorter than its diff:
```python
import functools
import math

import jax
import jax.numpy as jnp
from jax import lax
from jax.experimental import pallas as pl
from jax.experimental.pallas import tpu as pltpu
from jax.sharding import PartitionSpec as P

DK = 128
DV = 128
KERNEL = 4
HALO = 16
GROUP = 8
STEPS = 2
TILE = 256
MESH = pl.DeviceIdType.MESH
F32 = jnp.float32
BF16 = jnp.bfloat16
VMEM_LIMIT = 56 * 1024 * 1024
HIGHEST = lax.Precision.HIGHEST
NN = ((1,), (0,))
NT = ((1,), (1,))


def dot(a, b, dims=NN, precision=None):
    return lax.dot_general(a, b, (dims, ((), ())), preferred_element_type=F32, precision=precision)


def remote(src, dst, send, recv, ctx, head):
    return pltpu.make_async_remote_copy(
        src_ref=src, dst_ref=dst, send_sem=send, recv_sem=recv, device_id=(ctx, head), device_id_type=MESH
    )


def silu(x):
    return x / (1.0 + jnp.exp(-x))


def unit(feature, scale):
    norm = jnp.sum(feature * feature, -1, keepdims=True) + 1e-06
    return feature * (lax.rsqrt(norm) * scale)


def column(row):
    n = row.shape[1]
    same = lax.broadcasted_iota(jnp.int32, (n, n), 0) == lax.broadcasted_iota(jnp.int32, (n, n), 1)
    return jnp.sum(jnp.where(same, jnp.broadcast_to(row, (n, n)), 0.0), 1, keepdims=True)


def pair(both):
    n = both.shape[0]
    zero = jnp.zeros((n, n), both.dtype)
    return jnp.concatenate(
        [jnp.concatenate([both[:, :n], zero], 1), jnp.concatenate([zero, both[:, n:]], 1)], 0
    )


def invert(blocks):
    n = blocks[0].shape[0]
    row_at = lax.broadcasted_iota(jnp.int32, (n, 2 * n), 0)
    col_at = lax.broadcasted_iota(jnp.int32, (n, 2 * n), 1)
    differ = row_at ^ (col_at & (n - 1))
    one = jnp.where(differ == 0, 1.0, 0.0).astype(BF16)
    inverses = None
    width = 1
    while width < n:
        mask = jnp.where((differ >= width) & (differ < 2 * width), 1.0, 0.0).astype(BF16)
        lows = [block * mask for block in blocks]
        if inverses is None:
            inverses = [one - low for low in lows]
        else:
            right = [dot(low, pair(inv)).astype(BF16) for low, inv in zip(lows, inverses)]
            left = [dot(inv, pair(r)).astype(BF16) for inv, r in zip(inverses, right)]
            inverses = [inv - l for inv, l in zip(inverses, left)]
        width *= 2
    return inverses


def compose(later, earlier):
    return later + earlier + dot(later[:, :DK].astype(BF16), earlier.astype(BF16))


def kernel(
    groups, act, w_q, w_k, w_v, w_z, w_at, w_bt, cq, ck, cv, a_log, dt_bias, gain, w_o,
    out,
    ext, vq, vk, vv, vz, vo, pad, colt, rowt, inside, eff, gate, gated,
    maps, land, total, land2, pref, state, sbuf, s_in,
    part, relay, sums, reduced,
    lsem, hsend, hrecv, send1, recv1, send2, recv2, send3, recv3, rsend, rrecv, dsend, drecv,
):
    c = lax.axis_index("ctx")
    z = lax.axis_index("head")
    ctx = groups * GROUP
    g = c // GROUP
    me = lax.rem(c, GROUP)
    base = g * GROUP
    up, down, far = lax.rem(z + 1, 4), lax.rem(z + 3, 4), lax.rem(z + 2, 4)
    rows = act.shape[0]
    half = rows // 2
    heads = maps.shape[0]
    per = heads // STEPS
    kw, vw = w_q.shape[1] // STEPS, w_v.shape[1] // STEPS
    keys = w_q.shape[1]

    def fetch(step):
        ks, vs = pl.ds(step * kw, kw), pl.ds(step * vw, vw)
        return [
            pltpu.make_async_copy(w_q.at[:, ks], vq.at[:, ks], lsem.at[1 + 3 * step]),
            pltpu.make_async_copy(w_k.at[:, ks], vk.at[:, ks], lsem.at[2 + 3 * step]),
            pltpu.make_async_copy(w_v.at[:, vs], vv.at[:, vs], lsem.at[3 + 3 * step]),
        ]

    own = pltpu.make_async_copy(act, ext.at[pl.ds(HALO, rows)], lsem.at[0])
    last = 1 + 3 * STEPS
    tail_copies = [
        pltpu.make_async_copy(w_z, vz, lsem.at[last]),
        pltpu.make_async_copy(w_o, vo, lsem.at[last + 1]),
    ]
    own.start()
    for copy in fetch(0):
        copy.start()

    barrier = pltpu.get_barrier_semaphore()

    def greet(ctx_at, head_at):
        pl.semaphore_signal(barrier, inc=1, device_id=(ctx_at, head_at), device_id_type=MESH)

    for d in range(1, GROUP):
        greet(base + lax.rem(me + d, GROUP), z)
    for d in range(1, groups):
        greet(lax.rem(g + d, groups) * GROUP + me, z)
    greet(c, up)
    greet(c, down)

    @pl.when(me == 0)
    def _():
        greet(lax.rem(c + ctx - 1, ctx), z)

    pl.semaphore_wait(barrier, GROUP - 1 + groups - 1 + 2 + jnp.where(me == GROUP - 1, 1, 0))

    def halo(to):
        return remote(
            act.at[pl.ds(rows - HALO, HALO)], ext.at[pl.ds(0, HALO)], hsend, hrecv, to, z
        )

    @pl.when(c < ctx - 1)
    def _():
        halo(c + 1).start()

    @pl.when(c == 0)
    def _():
        ext[0:HALO] = jnp.zeros((HALO, ext.shape[1]), BF16)

    own.wait()
    tokens = ext[HALO:]
    beta = 1.0 / (1.0 + jnp.exp(-dot(w_bt[...], tokens, NT)))
    raw = dot(w_at[...], tokens, NT) + column(dt_bias[...])
    soft = jnp.maximum(raw, 0.0) + jnp.log1p(jnp.exp(-jnp.abs(raw)))
    logdecay = -jnp.exp(column(a_log[...])) * soft
    upto = (
        lax.broadcasted_iota(jnp.int32, (rows, rows), 0) <= lax.broadcasted_iota(jnp.int32, (rows, rows), 1)
    )
    cum = dot(logdecay, jnp.where(upto, 1.0, 0.0), NN, HIGHEST)
    rowt[...] = cum
    both = jnp.concatenate([cum, beta], 0)
    colt[...] = jnp.concatenate([both] * (128 // both.shape[0]), 0).T

    @pl.when(c > 0)
    def _():
        halo(c).wait_recv()

    row_at = lax.broadcasted_iota(jnp.int32, (half, half), 0)
    col_at = lax.broadcasted_iota(jnp.int32, (half, half), 1)
    lower = row_at >= col_at
    eye = jnp.where(
        lax.broadcasted_iota(jnp.int32, (DK, DK), 0) == lax.broadcasted_iota(jnp.int32, (DK, DK), 1), 1.0, 0.0
    )

    def project(weights, at, to):
        for n in range(0, at[1], TILE):
            out_n = dot(ext[...], weights[:, at[0] + n : at[0] + n + TILE])
            pad[:, to + n : to + n + TILE] = out_n.astype(BF16).astype(F32)

    def smooth(at, taps, taps_at):
        w = taps[:, taps_at : taps_at + DK]
        sum_ = w[KERNEL - 1 : KERNEL] * pad[HALO:, at : at + DK]
        for back in range(1, KERNEL):
            tap = w[KERNEL - 1 - back : KERNEL - back]
            sum_ = sum_ + tap * pad[HALO - back : HALO - back + rows, at : at + DK]
        return silu(sum_)

    for step in range(STEPS):
        for copy in fetch(step):
            copy.wait()
        for copy in fetch(step + 1) if step + 1 < STEPS else tail_copies:
            copy.start()
        project(vq, (step * kw, kw), step * kw)
        project(vk, (step * kw, kw), keys + step * kw)
        project(vv, (step * vw, vw), 2 * keys + step * vw)
        items = []
        for h in range(step * kw // DK, (step + 1) * kw // DK):
            query = unit(smooth(h * DK, cq, h * DK), 1.0 / math.sqrt(DK))
            key = unit(smooth(keys + h * DK, ck, h * DK), 1.0)
            kb = key.astype(BF16)
            gram = dot(jnp.concatenate([query.astype(BF16), kb], 0), kb, NT)
            qk, kk = gram[:rows], gram[rows:]
            key_t = key.T
            for j in range(2 * h, 2 * h + 2):
                value = smooth(2 * keys + j * DV, cv, j * DV)
                col = colt[:, j : j + 1]
                row = rowt[j : j + 1, :]
                b = colt[:, heads + j : heads + j + 1]
                f11 = jnp.exp(jnp.where(lower, col[:half] - row[:, :half], -1e30))
                f22 = jnp.exp(jnp.where(lower, col[half:] - row[:, half:], -1e30))
                f21 = jnp.exp(col[half:] - row[:, :half])
                a11 = (b[:half] * kk[:half, :half] * f11).astype(BF16)
                a22 = (b[half:] * kk[half:, half:] * f22).astype(BF16)
                a21 = (b[half:] * kk[half:, :half] * f21).astype(BF16)
                final = row[:, rows - 1 : rows]
                s1 = jnp.concatenate([qk[:half, :half] * f11, jnp.zeros((half, half), F32)], 1)
                s2 = jnp.concatenate([qk[half:, :half] * f21, qk[half:, half:] * f22], 1)
                left = jnp.concatenate([s1, s2, key_t * jnp.exp(final - row)], 0).astype(BF16)
                grow = jnp.exp(col)
                rhs = jnp.concatenate([key * (grow * b), value * b], 1).astype(BF16)
                items.append((j, jnp.concatenate([a11, a22], 1), a21, left, rhs, grow * query, final))
        inverses = invert([item[1] for item in items])
        for (j, _, a21, left, rhs, queries, final), inv in zip(items, inverses):
            x11, x22 = inv[:, :half], inv[:, half:]
            x21 = -dot(x22, dot(a21, x11).astype(BF16))
            whole = jnp.concatenate(
                [
                    jnp.concatenate([x11, jnp.zeros_like(x11)], 1),
                    jnp.concatenate([x21.astype(BF16), x22], 1),
                ],
                0,
            )
            wu = dot(whole, rhs).astype(BF16)
            res = dot(left, wu)
            at = slice(j * DV, (j + 1) * DV)
            inside[:, at] = res[:rows, DK:]
            eff[:, at] = (queries - res[:rows, :DK]).astype(BF16)
            first = (jnp.exp(final) - 1.0) * eye - res[rows:, :DK]
            maps[j] = jnp.concatenate([first, res[rows:, DK:]], 1).astype(BF16)
        for j in range(step * per, (step + 1) * per):

            @pl.when(j != me)
            def _(j=j):
                remote(maps.at[j], land.at[me], send1.at[j], recv1.at[me], base + j, z).start()

            @pl.when(j == me)
            def _(j=j):
                land[me] = maps[j]

    for copy in tail_copies:
        copy.wait()
    for n in range(0, gate.shape[1], TILE):
        raw_gate = dot(ext[HALO:], vz[:, n : n + TILE])
        gains = jnp.concatenate([gain[...]] * (TILE // DV), 1)
        gate[:, n : n + TILE] = silu(raw_gate) * gains

    for j in range(GROUP):

        @pl.when(j != me)
        def _(j=j):
            remote(maps.at[j], land.at[j], send1.at[j], recv1.at[j], base + j, z).wait_recv()

    m = [land[j].astype(F32) for j in range(GROUP)]
    p01, p23, p45, p67 = (compose(m[2 * k + 1], m[2 * k]) for k in range(4))
    p03, p47 = compose(p23, p01), compose(p67, p45)
    total[...] = compose(p47, p03).astype(BF16)
    for other in range(1, groups):

        @pl.when(g < other)
        def _(other=other):
            remote(total, land2.at[g], send2.at[other], recv2.at[g], other * GROUP + me, z).start()

    p05 = compose(p45, p03)
    for j, item in enumerate((m[0], p01, compose(m[2], p01), p03, compose(m[4], p03), p05, compose(m[6], p05))):
        pref[j] = item

    state[...] = jnp.zeros_like(state)
    for other in range(groups - 1):

        @pl.when(other < g)
        def _(other=other):
            remote(total, land2.at[other], send2.at[0], recv2.at[other], other * GROUP + me, z).wait_recv()
            now = state[...]
            step = land2[other]
            state[...] = now + step[:, DK:].astype(F32) + dot(step[:, :DK], now.astype(BF16))

    now = state[...]
    low = now.astype(BF16)
    for j in range(GROUP):
        if j == 0:
            sbuf[j] = low
        else:
            item = pref[j - 1]
            sbuf[j] = (now + item[:, DK:] + dot(item[:, :DK].astype(BF16), low)).astype(BF16)

        @pl.when(j != me)
        def _(j=j):
            remote(sbuf.at[j], s_in.at[me], send3.at[j], recv3.at[me], base + j, z).start()

    s_in[me] = sbuf[me]

    for j in range(heads):

        @pl.when(j != me)
        def _(j=j):
            remote(sbuf.at[j], s_in.at[j], send3.at[j], recv3.at[j], base + j, z).wait_recv()

        at = slice(j * DV, (j + 1) * DV)
        core = inside[:, at] + dot(eff[:, at], s_in[j])
        scale = lax.rsqrt(jnp.mean(core * core, -1, keepdims=True) + 1e-06)
        gated[:, at] = (core * scale * gate[:, at]).astype(BF16)

    width = part.shape[2] // 2
    lo, hi = slice(0, width), slice(width, 2 * width)
    relays = (
        remote(part.at[far, :, lo], relay.at[0], rsend.at[0], rrecv.at[0], c, up),
        remote(part.at[far, :, hi], relay.at[1], rsend.at[1], rrecv.at[1], c, down),
    )
    direct = (
        remote(part.at[down, :, lo], reduced.at[1, :, lo], dsend.at[0], drecv.at[0], c, down),
        remote(part.at[up, :, hi], reduced.at[0, :, hi], dsend.at[1], drecv.at[1], c, up),
    )
    summed = (
        remote(sums.at[0], reduced.at[0, :, lo], dsend.at[2], drecv.at[2], c, up),
        remote(sums.at[1], reduced.at[1, :, hi], dsend.at[3], drecv.at[3], c, down),
    )
    for k in range(2):
        for n in range(k * width, (k + 1) * width, TILE):
            tile = dot(gated[...], vo[:, n : n + TILE]).astype(BF16)
            part[:, :, n : n + TILE] = tile.reshape(part.shape[0], part.shape[1], TILE)
        relays[k].start()
        direct[k].start()
    for k, (peer, side) in enumerate(((up, lo), (down, hi))):
        relays[k].wait_recv()
        sums[k] = (part[peer, :, side].astype(F32) + relay[k].astype(F32)).astype(BF16)
        summed[k].start()
    for copy in direct + summed:
        copy.wait_recv()
    out[...] = (part[z].astype(F32) + reduced[0].astype(F32) + reduced[1].astype(F32)).astype(BF16)

    @pl.when(c < ctx - 1)
    def _():
        halo(c + 1).wait_send()

    for j in range(GROUP):

        @pl.when(j != me)
        def _(j=j):
            remote(maps.at[j], land.at[me], send1.at[j], recv1.at[me], base + j, z).wait_send()
            remote(sbuf.at[j], s_in.at[me], send3.at[j], recv3.at[me], base + j, z).wait_send()

    for other in range(1, groups):

        @pl.when(g < other)
        def _(other=other):
            remote(total, land2.at[g], send2.at[other], recv2.at[g], other * GROUP + me, z).wait_send()

    for copy in relays + direct + summed:
        copy.wait_send()


def local(
    activations, w_q, w_k, w_v, w_z, w_a, w_b, conv_q, conv_k, conv_v, a_log, dt_bias, norm_gain, w_o
):
    rows, depth = activations.shape
    heads = a_log.shape[0]
    groups = lax.axis_size("ctx") // GROUP
    parts = lax.axis_size("head")
    keys, values, wide = w_q.shape[1], w_v.shape[1], w_o.shape[1]
    hbm = pl.BlockSpec(memory_space=pl.ANY)
    vmem = pl.BlockSpec(memory_space=pltpu.VMEM)
    dma = pltpu.SemaphoreType.DMA
    piece = rows // parts
    return pl.pallas_call(
        functools.partial(kernel, groups),
        in_specs=[hbm] * 5 + [vmem] * 8 + [hbm],
        out_specs=vmem,
        out_shape=jax.ShapeDtypeStruct((piece, wide), BF16),
        scratch_shapes=[
            pltpu.VMEM((HALO + rows, depth), BF16),
            pltpu.VMEM(w_q.shape, BF16),
            pltpu.VMEM(w_k.shape, BF16),
            pltpu.VMEM(w_v.shape, BF16),
            pltpu.VMEM(w_z.shape, BF16),
            pltpu.VMEM(w_o.shape, BF16),
            pltpu.VMEM((HALO + rows, 2 * keys + values), F32),
            pltpu.VMEM((rows, 128), F32),
            pltpu.VMEM((heads, rows), F32),
            pltpu.VMEM((rows, values), F32),
            pltpu.VMEM((rows, heads * DK), BF16),
            pltpu.VMEM((rows, values), F32),
            pltpu.VMEM((rows, values), BF16),
            pltpu.VMEM((heads, DK, DK + DV), BF16),
            pltpu.VMEM((GROUP, DK, DK + DV), BF16),
            pltpu.VMEM((DK, DK + DV), BF16),
            pltpu.VMEM((groups, DK, DK + DV), BF16),
            pltpu.VMEM((GROUP, DK, DK + DV), F32),
            pltpu.VMEM((DK, DV), F32),
            pltpu.VMEM((GROUP, DK, DV), BF16),
            pltpu.VMEM((GROUP, DK, DV), BF16),
            pltpu.VMEM((parts, piece, wide), BF16),
            pltpu.VMEM((2, piece, wide // 2), BF16),
            pltpu.VMEM((2, piece, wide // 2), BF16),
            pltpu.VMEM((2, piece, wide), BF16),
            dma((3 + 3 * STEPS,)),
            dma,
            dma,
            dma((GROUP,)),
            dma((GROUP,)),
            dma((groups,)),
            dma((groups,)),
            dma((GROUP,)),
            dma((GROUP,)),
            dma((2,)),
            dma((2,)),
            dma((4,)),
            dma((4,)),
        ],
        compiler_params=pltpu.CompilerParams(
            collective_id=0, has_side_effects=True, vmem_limit_bytes=VMEM_LIMIT
        ),
        name="gated_delta_layer",
    )(
        activations, w_q, w_k, w_v, w_z, jnp.transpose(w_a), jnp.transpose(w_b), conv_q, conv_k, conv_v,
        a_log.reshape(1, -1), dt_bias.reshape(1, -1), norm_gain.reshape(1, -1), w_o,
    )


def solution(mesh):
    in_specs = (
        P("ctx", None),
        P(None, "head"),
        P(None, "head"),
        P(None, "head"),
        P(None, "head"),
        P(None, "head"),
        P(None, "head"),
        P(None, "head"),
        P(None, "head"),
        P(None, "head"),
        P("head"),
        P("head"),
        P(),
        P("head", None),
    )
    out_specs = P(("ctx", "head"), None)
    return jax.shard_map(local, mesh=mesh, in_specs=in_specs, out_specs=out_specs, check_vma=False)
```

time: 506 us -> 52.4 us (0.10)
  waiting for transfers between devices: 180 us -> 0 us
  other arithmetic: 164 us -> 0 us
  matrix products: 131 us -> 0 us
  Pallas kernels: 0 us -> 50.5 us
  between operations: 13.6 us -> 0.01 us
  local copies, waits for them, and re-layouts: 11.9 us -> 1.67 us
    another operation x7 -> x0, other arithmetic: 159 us -> none  [the longest x4 158 us: block_parts(): jax.scipy.linalg.solve_triangular(system, scaled, lower=True, unit_diagon...]
    all_gather x2 -> x0, waiting for transfers between devices: 147 us -> none  [entering(): pieces = jax.tree.map(lambda part: lax.all_gather(part, axis), value)]
    dot_general x60 -> x0, matrix products: 127 us -> none  [the longest x31 58.2 us: compose(): jnp.einsum('hde,hef->hdf', later[0], earlier[1], precision=highest)]
    pallas_call x0 -> x1, Pallas kernels: none -> 50.5 us  [local(): pl.pallas_call(functools.partial(kernel, groups), in_specs=[hbm] * 5 + [v...]
    reduce_scatter x1 -> x0, waiting for transfers between devices: 29.6 us -> none  [local(): lax.psum_scatter(jnp.dot(gated, w_o, preferred_element_type=jnp.float32),...]
    while x39 -> x0, local copies, waits for them, and re-layouts: 5.42 us -> none
  transfers between devices with their start and end apart: 4 -> 0, of which waited for: 4 -> 0; matrix products, arithmetic and copies ran while one was open for 0% -> 0% of each run, Pallas kernels for 0% -> 0%
where the time goes in v2:
time: 52.4 us; the launch traced here: 52.2 us
  Pallas kernels  50.5 us (96%)
  local copies, waits for them, and re-layouts  1.67 us (3%)
    pallas_call x1, Pallas kernels, local(): pl.pallas_call(functools.partial(kernel, groups), in_specs=[hbm] * 5 + [v...  50.5 us
    unnamed x1, local copies, waits for them, and re-layouts  1.67 us

profile of v2, /device:TPU:6, one launch (start us, length us, event | category | flops | bytes accessed | tf_op | source)
XLA Modules:
  0.0 52.2 jit_solution(10101665534539789797)
XLA Ops:
  0.0 50.5 %gated_delta_layer.1 = bf16[64,2048]{1,0:T(8,128)(2,1)} custom-call(bf16[256,2048]{1,0:T(8,128)(2,1)} %act.1, bf16[2048,512]{1,0:T(8,128)(2,1)} %w_q.1, bf16[2048,512]{1,0:T(8,128)(2,1)} %w_k.1, bf16[2048,1024]{1,0:T(8,128)(2,1)} %w_v.1, bf16[2048,1024]{1,0:T(8,128)(2,1)} %w_z.1, bf16[8,2048]{1,0:T(8,128)(2,1)} %bitcast.5, bf16[8,2048]{1,0:T(8,128)(2,1)} %bitcast.6, ...), custom_call_target="tpu_custom_call" | custom-call | tf_op jit(solution)/shard_map/gated_delta_layer/pallas_call | solution.py:380
  50.5 1.7 %copy.16 = bf16[64,2048]{1,0:T(8,128)(2,1)} copy(bf16[64,2048]{1,0:T(8,128)(2,1)} %gated_delta_layer.1) | data formatting | bytes 524288

commit v3 on v2

--- a/solution.py
+++ b/solution.py
@@ -57,7 +57,7 @@
     )
 
 
-def invert(blocks):
+def invert(blocks, found):
     n = blocks[0].shape[0]
     row_at = lax.broadcasted_iota(jnp.int32, (n, 2 * n), 0)
     col_at = lax.broadcasted_iota(jnp.int32, (n, 2 * n), 1)
@@ -72,10 +72,12 @@
             inverses = [one - low for low in lows]
         else:
             right = [dot(low, pair(inv)).astype(BF16) for low, inv in zip(lows, inverses)]
+            yield
             left = [dot(inv, pair(r)).astype(BF16) for inv, r in zip(inverses, right)]
             inverses = [inv - l for inv, l in zip(inverses, left)]
+            yield
         width *= 2
-    return inverses
+    found.extend(inverses)
 
 
 def compose(later, earlier):
@@ -119,7 +121,7 @@
         pltpu.make_async_copy(w_o, vo, lsem.at[last + 1]),
     ]
     own.start()
-    for copy in fetch(0):
+    for copy in fetch(0) + fetch(1):
         copy.start()
 
     barrier = pltpu.get_barrier_semaphore()
@@ -152,6 +154,17 @@
     @pl.when(c == 0)
     def _():
         ext[0:HALO] = jnp.zeros((HALO, ext.shape[1]), BF16)
+
+    def project(weights, n, to, first, count):
+        out_n = dot(ext[first : first + count], weights[:, n : n + TILE])
+        pad[first : first + count, to + n : to + n + TILE] = out_n.astype(BF16).astype(F32)
+
+    def projections(step, first, count):
+        todo = []
+        for weights, width, to in ((vq, kw, 0), (vk, kw, keys), (vv, vw, 2 * keys)):
+            for n in range(step * width, (step + 1) * width, TILE):
+                todo.append(functools.partial(project, weights, n, to, first, count))
+        return todo
 
     own.wait()
     tokens = ext[HALO:]
@@ -166,10 +179,19 @@
     rowt[...] = cum
     both = jnp.concatenate([cum, beta], 0)
     colt[...] = jnp.concatenate([both] * (128 // both.shape[0]), 0).T
+    for copy in fetch(0):
+        copy.wait()
+    for copy in tail_copies:
+        copy.start()
+    for work in projections(0, HALO, rows):
+        work()
 
     @pl.when(c > 0)
     def _():
         halo(c).wait_recv()
+
+    for work in projections(0, 0, HALO):
+        work()
 
     row_at = lax.broadcasted_iota(jnp.int32, (half, half), 0)
     col_at = lax.broadcasted_iota(jnp.int32, (half, half), 1)
@@ -177,11 +199,6 @@
     eye = jnp.where(
         lax.broadcasted_iota(jnp.int32, (DK, DK), 0) == lax.broadcasted_iota(jnp.int32, (DK, DK), 1), 1.0, 0.0
     )
-
-    def project(weights, at, to):
-        for n in range(0, at[1], TILE):
-            out_n = dot(ext[...], weights[:, at[0] + n : at[0] + n + TILE])
-            pad[:, to + n : to + n + TILE] = out_n.astype(BF16).astype(F32)
 
     def smooth(at, taps, taps_at):
         w = taps[:, taps_at : taps_at + DK]
@@ -191,58 +208,60 @@
             sum_ = sum_ + tap * pad[HALO - back : HALO - back + rows, at : at + DK]
         return silu(sum_)
 
-    for step in range(STEPS):
-        for copy in fetch(step):
-            copy.wait()
-        for copy in fetch(step + 1) if step + 1 < STEPS else tail_copies:
-            copy.start()
-        project(vq, (step * kw, kw), step * kw)
-        project(vk, (step * kw, kw), keys + step * kw)
-        project(vv, (step * vw, vw), 2 * keys + step * vw)
-        items = []
-        for h in range(step * kw // DK, (step + 1) * kw // DK):
-            query = unit(smooth(h * DK, cq, h * DK), 1.0 / math.sqrt(DK))
-            key = unit(smooth(keys + h * DK, ck, h * DK), 1.0)
-            kb = key.astype(BF16)
-            gram = dot(jnp.concatenate([query.astype(BF16), kb], 0), kb, NT)
-            qk, kk = gram[:rows], gram[rows:]
-            key_t = key.T
-            for j in range(2 * h, 2 * h + 2):
-                value = smooth(2 * keys + j * DV, cv, j * DV)
-                col = colt[:, j : j + 1]
-                row = rowt[j : j + 1, :]
-                b = colt[:, heads + j : heads + j + 1]
-                f11 = jnp.exp(jnp.where(lower, col[:half] - row[:, :half], -1e30))
-                f22 = jnp.exp(jnp.where(lower, col[half:] - row[:, half:], -1e30))
-                f21 = jnp.exp(col[half:] - row[:, :half])
-                a11 = (b[:half] * kk[:half, :half] * f11).astype(BF16)
-                a22 = (b[half:] * kk[half:, half:] * f22).astype(BF16)
-                a21 = (b[half:] * kk[half:, :half] * f21).astype(BF16)
-                final = row[:, rows - 1 : rows]
-                s1 = jnp.concatenate([qk[:half, :half] * f11, jnp.zeros((half, half), F32)], 1)
-                s2 = jnp.concatenate([qk[half:, :half] * f21, qk[half:, half:] * f22], 1)
-                left = jnp.concatenate([s1, s2, key_t * jnp.exp(final - row)], 0).astype(BF16)
-                grow = jnp.exp(col)
-                rhs = jnp.concatenate([key * (grow * b), value * b], 1).astype(BF16)
-                items.append((j, jnp.concatenate([a11, a22], 1), a21, left, rhs, grow * query, final))
-        inverses = invert([item[1] for item in items])
-        for (j, _, a21, left, rhs, queries, final), inv in zip(items, inverses):
-            x11, x22 = inv[:, :half], inv[:, half:]
-            x21 = -dot(x22, dot(a21, x11).astype(BF16))
-            whole = jnp.concatenate(
+    def prepare(h, items):
+        query = unit(smooth(h * DK, cq, h * DK), 1.0 / math.sqrt(DK))
+        key = unit(smooth(keys + h * DK, ck, h * DK), 1.0)
+        kb = key.astype(BF16)
+        gram = dot(jnp.concatenate([query.astype(BF16), kb], 0), kb, NT)
+        qk, kk = gram[:rows], gram[rows:]
+        key_t = key.T
+        for j in range(2 * h, 2 * h + 2):
+            value = smooth(2 * keys + j * DV, cv, j * DV)
+            col = colt[:, j : j + 1]
+            row = rowt[j : j + 1, :]
+            b = colt[:, heads + j : heads + j + 1]
+            f11 = jnp.exp(jnp.where(lower, col[:half] - row[:, :half], -1e30))
+            f22 = jnp.exp(jnp.where(lower, col[half:] - row[:, half:], -1e30))
+            f21 = jnp.exp(col[half:] - row[:, :half])
+            a11 = (b[:half] * kk[:half, :half] * f11).astype(BF16)
+            a22 = (b[half:] * kk[half:, half:] * f22).astype(BF16)
+            a21 = (b[half:] * kk[half:, :half] * f21).astype(BF16)
+            final = row[:, rows - 1 : rows]
+            s1 = jnp.concatenate([qk[:half, :half] * f11, jnp.zeros((half, half), F32)], 1)
+            s2 = jnp.concatenate([qk[half:, :half] * f21, qk[half:, half:] * f22], 1)
+            left = jnp.concatenate([s1, s2, key_t * jnp.exp(final - row)], 0).astype(BF16)
+            grow = jnp.exp(col)
+            rhs = jnp.concatenate([key * (grow * b), value * b], 1).astype(BF16)
+            items.append((j, jnp.concatenate([a11, a22], 1), a21, left, rhs, grow * query, final))
+
+    def conclude(items, inverses):
+        halves = [(inv[:, :half], inv[:, half:]) for inv in inverses]
+        lows = [dot(item[2], x11).astype(BF16) for item, (x11, _) in zip(items, halves)]
+        yield
+        corners = [-dot(x22, low) for low, (_, x22) in zip(lows, halves)]
+        wholes = [
+            jnp.concatenate(
                 [
                     jnp.concatenate([x11, jnp.zeros_like(x11)], 1),
                     jnp.concatenate([x21.astype(BF16), x22], 1),
                 ],
                 0,
             )
-            wu = dot(whole, rhs).astype(BF16)
-            res = dot(left, wu)
+            for x21, (x11, x22) in zip(corners, halves)
+        ]
+        yield
+        solved = [dot(whole, item[4]).astype(BF16) for item, whole in zip(items, wholes)]
+        yield
+        results = [dot(item[3], wu) for item, wu in zip(items, solved)]
+        for (j, _, _, _, _, queries, final), res in zip(items, results):
+            first = (jnp.exp(final) - 1.0) * eye - res[rows:, :DK]
+            maps[j] = jnp.concatenate([first, res[rows:, DK:]], 1).astype(BF16)
             at = slice(j * DV, (j + 1) * DV)
             inside[:, at] = res[:rows, DK:]
             eff[:, at] = (queries - res[:rows, :DK]).astype(BF16)
-            first = (jnp.exp(final) - 1.0) * eye - res[rows:, :DK]
-            maps[j] = jnp.concatenate([first, res[rows:, DK:]], 1).astype(BF16)
+        yield
+
+    def dispatch(step):
         for j in range(step * per, (step + 1) * per):
 
             @pl.when(j != me)
@@ -252,6 +271,26 @@
             @pl.when(j == me)
             def _(j=j):
                 land[me] = maps[j]
+
+    key_heads = kw // DK
+    early, later = [], []
+    for h in range(key_heads):
+        prepare(h, early)
+    for copy in fetch(1):
+        copy.wait()
+    for work in projections(1, 0, HALO + rows):
+        work()
+    for h in range(key_heads, 2 * key_heads):
+        prepare(h, later)
+    found = []
+    for _ in invert([item[1] for item in early + later], found):
+        pass
+    for _ in conclude(early, found[:per]):
+        pass
+    dispatch(0)
+    for _ in conclude(later, found[per:]):
+        pass
+    dispatch(1)
 
     for copy in tail_copies:
         copy.wait()
@@ -270,18 +309,36 @@
     p01, p23, p45, p67 = (compose(m[2 * k + 1], m[2 * k]) for k in range(4))
     p03, p47 = compose(p23, p01), compose(p67, p45)
     total[...] = compose(p47, p03).astype(BF16)
+
+    def first_total(other):
+        return remote(
+            total.at[:, pl.ds(DK, DV)], land2.at[0, :, pl.ds(DK, DV)], send2.at[other], recv2.at[0],
+            other * GROUP + me, z,
+        )
+
     for other in range(1, groups):
 
-        @pl.when(g < other)
+        @pl.when((g > 0) & (g < other))
         def _(other=other):
             remote(total, land2.at[g], send2.at[other], recv2.at[g], other * GROUP + me, z).start()
 
+        @pl.when(g == 0)
+        def _(other=other):
+            first_total(other).start()
+
     p05 = compose(p45, p03)
+    pref[0] = jnp.zeros((DK, DK + DV), F32)
     for j, item in enumerate((m[0], p01, compose(m[2], p01), p03, compose(m[4], p03), p05, compose(m[6], p05))):
-        pref[j] = item
+        pref[j + 1] = item
 
     state[...] = jnp.zeros_like(state)
-    for other in range(groups - 1):
+
+    @pl.when(g > 0)
+    def _():
+        first_total(0).wait_recv()
+        state[...] = land2[0, :, DK:].astype(F32)
+
+    for other in range(1, groups - 1):
 
         @pl.when(other < g)
         def _(other=other):
@@ -292,29 +349,35 @@
 
     now = state[...]
     low = now.astype(BF16)
-    for j in range(GROUP):
-        if j == 0:
-            sbuf[j] = low
-        else:
-            item = pref[j - 1]
-            sbuf[j] = (now + item[:, DK:] + dot(item[:, :DK].astype(BF16), low)).astype(BF16)
-
-        @pl.when(j != me)
-        def _(j=j):
-            remote(sbuf.at[j], s_in.at[me], send3.at[j], recv3.at[me], base + j, z).start()
-
+
+    def enter(j):
+        item = pref[j]
+        sbuf[j] = (now + item[:, DK:] + dot(item[:, :DK].astype(BF16), low)).astype(BF16)
+
+    def entered(peer):
+        return remote(sbuf.at[peer], s_in.at[me], send3.at[peer], recv3.at[me], base + peer, z)
+
+    for batch in ((4, 5, 3, 6), (2, 7, 1, 0)):
+        peers = [lax.rem(me + d, GROUP) for d in batch]
+        for peer in peers:
+            enter(peer)
+        for d, peer in zip(batch, peers):
+            if d:
+                entered(peer).start()
     s_in[me] = sbuf[me]
 
-    for j in range(heads):
-
-        @pl.when(j != me)
-        def _(j=j):
-            remote(sbuf.at[j], s_in.at[j], send3.at[j], recv3.at[j], base + j, z).wait_recv()
-
-        at = slice(j * DV, (j + 1) * DV)
-        core = inside[:, at] + dot(eff[:, at], s_in[j])
-        scale = lax.rsqrt(jnp.mean(core * core, -1, keepdims=True) + 1e-06)
-        gated[:, at] = (core * scale * gate[:, at]).astype(BF16)
+    for batch in ((0, 1, 7), (2, 6), (3, 5, 4)):
+        members = [lax.rem(me + d, GROUP) for d in batch]
+        for d, j in zip(batch, members):
+            if d:
+                remote(sbuf.at[j], s_in.at[j], send3.at[j], recv3.at[j], base + j, z).wait_recv()
+        cores = []
+        for j in members:
+            at = pl.ds(pl.multiple_of(j * DV, DV), DV)
+            cores.append((at, inside[:, at] + dot(eff[:, at], s_in[j])))
+        for at, core in cores:
+            scale = lax.rsqrt(jnp.mean(core * core, -1, keepdims=True) + 1e-06)
+            gated[:, at] = (core * scale * gate[:, at]).astype(BF16)
 
     width = part.shape[2] // 2
     lo, hi = slice(0, width), slice(width, 2 * width)
@@ -357,9 +420,13 @@
 
     for other in range(1, groups):
 
-        @pl.when(g < other)
+        @pl.when((g > 0) & (g < other))
         def _(other=other):
             remote(total, land2.at[g], send2.at[other], recv2.at[g], other * GROUP + me, z).wait_send()
+
+        @pl.when(g == 0)
+        def _(other=other):
+            first_total(other).wait_send()
 
     for copy in relays + direct + summed:
         copy.wait_send()
@@ -381,7 +448,7 @@
         functools.partial(kernel, groups),
         in_specs=[hbm] * 5 + [vmem] * 8 + [hbm],
         out_specs=vmem,
-        out_shape=jax.ShapeDtypeStruct((piece, wide), BF16),
+        out_shape=pltpu.VMEM((piece, wide), BF16),
         scratch_shapes=[
             pltpu.VMEM((HALO + rows, depth), BF16),
             pltpu.VMEM(w_q.shape, BF16),

time: 52.4 us -> 47.3 us (0.903)
  Pallas kernels: 50.5 us -> 46.2 us
  local copies, waits for them, and re-layouts: 1.67 us -> 0.71 us
    pallas_call x1, Pallas kernels: 50.5 us -> 46.2 us  [local(): pl.pallas_call(functools.partial(kernel, groups), in_specs=[hbm] * 5 + [v...]
    unnamed x1, local copies, waits for them, and re-layouts: 1.67 us -> 0.71 us
where the time goes in v3:
time: 47.3 us; the launch traced here: 46.9 us
  Pallas kernels  46.2 us (98%)
  local copies, waits for them, and re-layouts  0.71 us (2%)
    pallas_call x1, Pallas kernels, local(): pl.pallas_call(functools.partial(kernel, groups), in_specs=[hbm] * 5 + [v...  46.2 us

profile of v3, /device:TPU:6, one launch (start us, length us, event | category | flops | bytes accessed | tf_op | source)
XLA Modules:
  0.0 46.9 jit_solution(9894809852752332051)
XLA Ops:
  0.0 46.2 %gated_delta_layer.1 = bf16[64,2048]{1,0:T(8,128)(2,1)S(1)} custom-call(bf16[256,2048]{1,0:T(8,128)(2,1)} %act.1, bf16[2048,512]{1,0:T(8,128)(2,1)} %w_q.1, bf16[2048,512]{1,0:T(8,128)(2,1)} %w_k.1, bf16[2048,1024]{1,0:T(8,128)(2,1)} %w_v.1, bf16[2048,1024]{1,0:T(8,128)(2,1)} %w_z.1, bf16[8,2048]{1,0:T(8,128)(2,1)} %bitcast.5, bf16[8,2048]{1,0:T(8,128)(2,1)} %bitcast.6, ...), custom_call_target="tpu_custom_call" | custom-call | tf_op jit(solution)/shard_map/gated_delta_layer/pallas_call | solution.py:447
  46.2 0.7 %copy.16 = bf16[64,2048]{1,0:T(8,128)(2,1)} copy(bf16[64,2048]{1,0:T(8,128)(2,1)S(1)} %gated_delta_layer.1) | data formatting | bytes 524288

commit v4 on v3

--- a/solution.py
+++ b/solution.py
@@ -87,7 +87,7 @@
 def kernel(
     groups, act, w_q, w_k, w_v, w_z, w_at, w_bt, cq, ck, cv, a_log, dt_bias, gain, w_o,
     out,
-    ext, vq, vk, vv, vz, vo, pad, colt, rowt, inside, eff, gate, gated,
+    ext, vq, vk, vv, vz, vo, pad, colt, rowt, keyb, solutions, inside, eff, gate, gated,
     maps, land, total, land2, pref, state, sbuf, s_in,
     part, relay, sums, reduced,
     lsem, hsend, hrecv, send1, recv1, send2, recv2, send3, recv3, rsend, rrecv, dsend, drecv,
@@ -109,16 +109,16 @@
     def fetch(step):
         ks, vs = pl.ds(step * kw, kw), pl.ds(step * vw, vw)
         return [
-            pltpu.make_async_copy(w_q.at[:, ks], vq.at[:, ks], lsem.at[1 + 3 * step]),
-            pltpu.make_async_copy(w_k.at[:, ks], vk.at[:, ks], lsem.at[2 + 3 * step]),
-            pltpu.make_async_copy(w_v.at[:, vs], vv.at[:, vs], lsem.at[3 + 3 * step]),
+            pltpu.make_async_copy(w_k.at[:, ks], vk.at[:, ks], lsem.at[1 + 2 * step]),
+            pltpu.make_async_copy(w_v.at[:, vs], vv.at[:, vs], lsem.at[2 + 2 * step]),
         ]
 
     own = pltpu.make_async_copy(act, ext.at[pl.ds(HALO, rows)], lsem.at[0])
-    last = 1 + 3 * STEPS
+    last = 1 + 2 * STEPS
     tail_copies = [
-        pltpu.make_async_copy(w_z, vz, lsem.at[last]),
-        pltpu.make_async_copy(w_o, vo, lsem.at[last + 1]),
+        pltpu.make_async_copy(w_q, vq, lsem.at[last]),
+        pltpu.make_async_copy(w_z, vz, lsem.at[last + 1]),
+        pltpu.make_async_copy(w_o, vo, lsem.at[last + 2]),
     ]
     own.start()
     for copy in fetch(0) + fetch(1):
@@ -161,7 +161,7 @@
 
     def projections(step, first, count):
         todo = []
-        for weights, width, to in ((vq, kw, 0), (vk, kw, keys), (vv, vw, 2 * keys)):
+        for weights, width, to in ((vk, kw, keys), (vv, vw, 2 * keys)):
             for n in range(step * width, (step + 1) * width, TILE):
                 todo.append(functools.partial(project, weights, n, to, first, count))
         return todo
@@ -208,31 +208,31 @@
             sum_ = sum_ + tap * pad[HALO - back : HALO - back + rows, at : at + DK]
         return silu(sum_)
 
+    def factors(j):
+        col, row = colt[:, j : j + 1], rowt[j : j + 1, :]
+        f11 = jnp.exp(jnp.where(lower, col[:half] - row[:, :half], -1e30))
+        f22 = jnp.exp(jnp.where(lower, col[half:] - row[:, half:], -1e30))
+        f21 = jnp.exp(col[half:] - row[:, :half])
+        return f11, f22, f21
+
     def prepare(h, items):
-        query = unit(smooth(h * DK, cq, h * DK), 1.0 / math.sqrt(DK))
         key = unit(smooth(keys + h * DK, ck, h * DK), 1.0)
         kb = key.astype(BF16)
-        gram = dot(jnp.concatenate([query.astype(BF16), kb], 0), kb, NT)
-        qk, kk = gram[:rows], gram[rows:]
+        keyb[:, h * DK : (h + 1) * DK] = kb
+        kk = dot(kb, kb, NT)
         key_t = key.T
         for j in range(2 * h, 2 * h + 2):
             value = smooth(2 * keys + j * DV, cv, j * DV)
-            col = colt[:, j : j + 1]
+            f11, f22, f21 = factors(j)
+            b = colt[:, heads + j : heads + j + 1]
             row = rowt[j : j + 1, :]
-            b = colt[:, heads + j : heads + j + 1]
-            f11 = jnp.exp(jnp.where(lower, col[:half] - row[:, :half], -1e30))
-            f22 = jnp.exp(jnp.where(lower, col[half:] - row[:, half:], -1e30))
-            f21 = jnp.exp(col[half:] - row[:, :half])
             a11 = (b[:half] * kk[:half, :half] * f11).astype(BF16)
             a22 = (b[half:] * kk[half:, half:] * f22).astype(BF16)
             a21 = (b[half:] * kk[half:, :half] * f21).astype(BF16)
             final = row[:, rows - 1 : rows]
-            s1 = jnp.concatenate([qk[:half, :half] * f11, jnp.zeros((half, half), F32)], 1)
-            s2 = jnp.concatenate([qk[half:, :half] * f21, qk[half:, half:] * f22], 1)
-            left = jnp.concatenate([s1, s2, key_t * jnp.exp(final - row)], 0).astype(BF16)
-            grow = jnp.exp(col)
-            rhs = jnp.concatenate([key * (grow * b), value * b], 1).astype(BF16)
-            items.append((j, jnp.concatenate([a11, a22], 1), a21, left, rhs, grow * query, final))
+            carried = (key_t * jnp.exp(final - row)).astype(BF16)
+            rhs = jnp.concatenate([key * (jnp.exp(colt[:, j : j + 1]) * b), value * b], 1).astype(BF16)
+            items.append((j, jnp.concatenate([a11, a22], 1), a21, carried, rhs, final))
 
     def conclude(items, inverses):
         halves = [(inv[:, :half], inv[:, half:]) for inv in inverses]
@@ -253,12 +253,10 @@
         solved = [dot(whole, item[4]).astype(BF16) for item, whole in zip(items, wholes)]
         yield
         results = [dot(item[3], wu) for item, wu in zip(items, solved)]
-        for (j, _, _, _, _, queries, final), res in zip(items, results):
-            first = (jnp.exp(final) - 1.0) * eye - res[rows:, :DK]
-            maps[j] = jnp.concatenate([first, res[rows:, DK:]], 1).astype(BF16)
-            at = slice(j * DV, (j + 1) * DV)
-            inside[:, at] = res[:rows, DK:]
-            eff[:, at] = (queries - res[:rows, :DK]).astype(BF16)
+        for (j, _, _, _, _, final), res, wu in zip(items, results, solved):
+            first = (jnp.exp(final) - 1.0) * eye - res[:, :DK]
+            maps[j] = jnp.concatenate([first, res[:, DK:]], 1).astype(BF16)
+            solutions[j] = wu
         yield
 
     def dispatch(step):
@@ -292,12 +290,33 @@
         pass
     dispatch(1)
 
-    for copy in tail_copies:
-        copy.wait()
-    for n in range(0, gate.shape[1], TILE):
-        raw_gate = dot(ext[HALO:], vz[:, n : n + TILE])
-        gains = jnp.concatenate([gain[...]] * (TILE // DV), 1)
-        gate[:, n : n + TILE] = silu(raw_gate) * gains
+    tail_copies[0].wait()
+    for n in range(0, keys, TILE):
+        project(vq, n, 0, 0, HALO + rows)
+    scores = []
+    for h in range(keys // DK):
+        query = unit(smooth(h * DK, cq, h * DK), 1.0 / math.sqrt(DK))
+        qk = dot(query.astype(BF16), keyb[:, h * DK : (h + 1) * DK], NT)
+        for j in range(2 * h, 2 * h + 2):
+            f11, f22, f21 = factors(j)
+            s1 = jnp.concatenate([qk[:half, :half] * f11, jnp.zeros((half, half), F32)], 1)
+            s2 = jnp.concatenate([qk[half:, :half] * f21, qk[half:, half:] * f22], 1)
+            both = jnp.concatenate([s1, s2], 0).astype(BF16)
+            scores.append((both, jnp.exp(colt[:, j : j + 1]) * query))
+    for j, (both, queries) in enumerate(scores):
+        res = dot(both, solutions[j])
+        at = slice(j * DV, (j + 1) * DV)
+        inside[:, at] = res[:, DK:]
+        eff[:, at] = (queries - res[:, :DK]).astype(BF16)
+
+    def gates(first, stop):
+        for n in range(first, stop, TILE):
+            raw_gate = dot(ext[HALO:], vz[:, n : n + TILE])
+            gains = jnp.concatenate([gain[...]] * (TILE // DV), 1)
+            gate[:, n : n + TILE] = silu(raw_gate) * gains
+
+    tail_copies[1].wait()
+    gates(0, gate.shape[1] // 2)
 
     for j in range(GROUP):
 
@@ -332,6 +351,8 @@
         pref[j + 1] = item
 
     state[...] = jnp.zeros_like(state)
+    gates(gate.shape[1] // 2, gate.shape[1])
+    tail_copies[2].wait()
 
     @pl.when(g > 0)
     def _():
@@ -459,6 +480,8 @@
             pltpu.VMEM((HALO + rows, 2 * keys + values), F32),
             pltpu.VMEM((rows, 128), F32),
             pltpu.VMEM((heads, rows), F32),
+            pltpu.VMEM((rows, keys), BF16),
+            pltpu.VMEM((heads, rows, DK + DV), BF16),
             pltpu.VMEM((rows, values), F32),
             pltpu.VMEM((rows, heads * DK), BF16),
             pltpu.VMEM((rows, values), F32),
@@ -475,7 +498,7 @@
             pltpu.VMEM((2, piece, wide // 2), BF16),
             pltpu.VMEM((2, piece, wide // 2), BF16),
             pltpu.VMEM((2, piece, wide), BF16),
-            dma((3 + 3 * STEPS,)),
+            dma((4 + 2 * STEPS,)),
             dma,
             dma,
             dma((GROUP,)),

time: 47.3 us -> 45.8 us (0.968)
  Pallas kernels: 46.2 us -> 44.7 us
    pallas_call x1, Pallas kernels: 46.2 us -> 44.7 us  [local(): pl.pallas_call(functools.partial(kernel, groups), in_specs=[hbm] * 5 + [v...]
where the time goes in v4:
time: 45.8 us; the launch traced here: 45.4 us
  Pallas kernels  44.7 us (98%)
  local copies, waits for them, and re-layouts  0.71 us (2%)
    pallas_call x1, Pallas kernels, local(): pl.pallas_call(functools.partial(kernel, groups), in_specs=[hbm] * 5 + [v...  44.7 us

profile of v4, /device:TPU:6, one launch (start us, length us, event | category | flops | bytes accessed | tf_op | source)
XLA Modules:
  0.0 45.4 jit_solution(4150959512705277487)
XLA Ops:
  0.0 44.7 %gated_delta_layer.1 = bf16[64,2048]{1,0:T(8,128)(2,1)S(1)} custom-call(bf16[256,2048]{1,0:T(8,128)(2,1)} %act.1, bf16[2048,512]{1,0:T(8,128)(2,1)} %w_q.1, bf16[2048,512]{1,0:T(8,128)(2,1)} %w_k.1, bf16[2048,1024]{1,0:T(8,128)(2,1)} %w_v.1, bf16[2048,1024]{1,0:T(8,128)(2,1)} %w_z.1, bf16[8,2048]{1,0:T(8,128)(2,1)} %bitcast.5, bf16[8,2048]{1,0:T(8,128)(2,1)} %bitcast.6, ...), custom_call_target="tpu_custom_call" | custom-call | tf_op jit(solution)/shard_map/gated_delta_layer/pallas_call | solution.py:468
  44.7 0.7 %copy.16 = bf16[64,2048]{1,0:T(8,128)(2,1)} copy(bf16[64,2048]{1,0:T(8,128)(2,1)S(1)} %gated_delta_layer.1) | data formatting | bytes 524288

commit v5 on v4

--- a/solution.py
+++ b/solution.py
@@ -49,12 +49,9 @@
     return jnp.sum(jnp.where(same, jnp.broadcast_to(row, (n, n)), 0.0), 1, keepdims=True)
 
 
-def pair(both):
-    n = both.shape[0]
-    zero = jnp.zeros((n, n), both.dtype)
-    return jnp.concatenate(
-        [jnp.concatenate([both[:, :n], zero], 1), jnp.concatenate([zero, both[:, n:]], 1)], 0
-    )
+def each(a, b):
+    n = a.shape[0]
+    return jnp.concatenate([dot(a[:, :n], b[:, :n]), dot(a[:, n:], b[:, n:])], 1)
 
 
 def invert(blocks, found):
@@ -71,9 +68,9 @@
         if inverses is None:
             inverses = [one - low for low in lows]
         else:
-            right = [dot(low, pair(inv)).astype(BF16) for low, inv in zip(lows, inverses)]
+            right = [each(low, inv).astype(BF16) for low, inv in zip(lows, inverses)]
             yield
-            left = [dot(inv, pair(r)).astype(BF16) for inv, r in zip(inverses, right)]
+            left = [each(inv, r).astype(BF16) for inv, r in zip(inverses, right)]
             inverses = [inv - l for inv, l in zip(inverses, left)]
             yield
         width *= 2
@@ -259,14 +256,22 @@
             solutions[j] = wu
         yield
 
+    def owner(j):
+        return 2 * (j % per) + j // per
+
+    def owned(member):
+        return member // 2 + per * lax.rem(member, 2)
+
+    mine = owned(me)
+
     def dispatch(step):
         for j in range(step * per, (step + 1) * per):
 
-            @pl.when(j != me)
+            @pl.when(owner(j) != me)
             def _(j=j):
-                remote(maps.at[j], land.at[me], send1.at[j], recv1.at[me], base + j, z).start()
-
-            @pl.when(j == me)
+                remote(maps.at[j], land.at[me], send1.at[j], recv1.at[me], base + owner(j), z).start()
+
+            @pl.when(owner(j) == me)
             def _(j=j):
                 land[me] = maps[j]
 
@@ -376,7 +381,7 @@
         sbuf[j] = (now + item[:, DK:] + dot(item[:, :DK].astype(BF16), low)).astype(BF16)
 
     def entered(peer):
-        return remote(sbuf.at[peer], s_in.at[me], send3.at[peer], recv3.at[me], base + peer, z)
+        return remote(sbuf.at[peer], s_in.at[mine], send3.at[peer], recv3.at[mine], base + peer, z)
 
     for batch in ((4, 5, 3, 6), (2, 7, 1, 0)):
         peers = [lax.rem(me + d, GROUP) for d in batch]
@@ -385,15 +390,16 @@
         for d, peer in zip(batch, peers):
             if d:
                 entered(peer).start()
-    s_in[me] = sbuf[me]
+    s_in[mine] = sbuf[me]
 
     for batch in ((0, 1, 7), (2, 6), (3, 5, 4)):
         members = [lax.rem(me + d, GROUP) for d in batch]
-        for d, j in zip(batch, members):
+        cores = []
+        for d, peer in zip(batch, members):
             if d:
-                remote(sbuf.at[j], s_in.at[j], send3.at[j], recv3.at[j], base + j, z).wait_recv()
-        cores = []
-        for j in members:
+                j = owned(peer)
+                remote(sbuf.at[peer], s_in.at[j], send3.at[peer], recv3.at[j], base + peer, z).wait_recv()
+        for j in map(owned, members):
             at = pl.ds(pl.multiple_of(j * DV, DV), DV)
             cores.append((at, inside[:, at] + dot(eff[:, at], s_in[j])))
         for at, core in cores:
@@ -424,30 +430,33 @@
         relays[k].wait_recv()
         sums[k] = (part[peer, :, side].astype(F32) + relay[k].astype(F32)).astype(BF16)
         summed[k].start()
+    @pl.when(c < ctx - 1)
+    def _():
+        halo(c + 1).wait_send()
+
+    for j in range(GROUP):
+
+        @pl.when(owner(j) != me)
+        def _(j=j):
+            remote(maps.at[j], land.at[me], send1.at[j], recv1.at[me], base + owner(j), z).wait_send()
+
+        @pl.when(j != me)
+        def _(j=j):
+            entered(j).wait_send()
+
+    for other in range(1, groups):
+
+        @pl.when((g > 0) & (g < other))
+        def _(other=other):
+            remote(total, land2.at[g], send2.at[other], recv2.at[g], other * GROUP + me, z).wait_send()
+
+        @pl.when(g == 0)
+        def _(other=other):
+            first_total(other).wait_send()
+
     for copy in direct + summed:
         copy.wait_recv()
     out[...] = (part[z].astype(F32) + reduced[0].astype(F32) + reduced[1].astype(F32)).astype(BF16)
-
-    @pl.when(c < ctx - 1)
-    def _():
-        halo(c + 1).wait_send()
-
-    for j in range(GROUP):
-
-        @pl.when(j != me)
-        def _(j=j):
-            remote(maps.at[j], land.at[me], send1.at[j], recv1.at[me], base + j, z).wait_send()
-            remote(sbuf.at[j], s_in.at[me], send3.at[j], recv3.at[me], base + j, z).wait_send()
-
-    for other in range(1, groups):
-
-        @pl.when((g > 0) & (g < other))
-        def _(other=other):
-            remote(total, land2.at[g], send2.at[other], recv2.at[g], other * GROUP + me, z).wait_send()
-
-        @pl.when(g == 0)
-        def _(other=other):
-            first_total(other).wait_send()
 
     for copy in relays + direct + summed:
         copy.wait_send()

time: 45.8 us -> 45 us (0.983)
  Pallas kernels: 44.7 us -> 43.9 us
    pallas_call x1, Pallas kernels: 44.7 us -> 43.9 us  [local(): pl.pallas_call(functools.partial(kernel, groups), in_specs=[hbm] * 5 + [v...]
where the time goes in v5:
time: 45 us; the launch traced here: 44.7 us
  Pallas kernels  43.9 us (98%)
  local copies, waits for them, and re-layouts  0.71 us (2%)
    pallas_call x1, Pallas kernels, local(): pl.pallas_call(functools.partial(kernel, groups), in_specs=[hbm] * 5 + [v...  43.9 us

profile of v5, /device:TPU:6, one launch (start us, length us, event | category | flops | bytes accessed | tf_op | source)
XLA Modules:
  0.0 44.7 jit_solution(16116628112902439736)
XLA Ops:
  0.0 43.9 %gated_delta_layer.1 = bf16[64,2048]{1,0:T(8,128)(2,1)S(1)} custom-call(bf16[256,2048]{1,0:T(8,128)(2,1)} %act.1, bf16[2048,512]{1,0:T(8,128)(2,1)} %w_q.1, bf16[2048,512]{1,0:T(8,128)(2,1)} %w_k.1, bf16[2048,1024]{1,0:T(8,128)(2,1)} %w_v.1, bf16[2048,1024]{1,0:T(8,128)(2,1)} %w_z.1, bf16[8,2048]{1,0:T(8,128)(2,1)} %bitcast.5, bf16[8,2048]{1,0:T(8,128)(2,1)} %bitcast.6, ...), custom_call_target="tpu_custom_call" | custom-call | tf_op jit(solution)/shard_map/gated_delta_layer/pallas_call | solution.py:477
  44.0 0.7 %copy.16 = bf16[64,2048]{1,0:T(8,128)(2,1)} copy(bf16[64,2048]{1,0:T(8,128)(2,1)S(1)} %gated_delta_layer.1) | data formatting | bytes 524288

commit v6 on v5

--- a/solution.py
+++ b/solution.py
@@ -454,9 +454,14 @@
         def _(other=other):
             first_total(other).wait_send()
 
-    for copy in direct + summed:
-        copy.wait_recv()
-    out[...] = (part[z].astype(F32) + reduced[0].astype(F32) + reduced[1].astype(F32)).astype(BF16)
+    piece = out.shape[0]
+    tops = (slice(0, piece), slice(piece, 2 * piece))
+    for k, side in enumerate((lo, hi)):
+        direct[k].wait_recv()
+        inside[tops[k]] = part[z, :, side].astype(F32) + reduced[1 - k, :, side].astype(F32)
+    for k, side in enumerate((lo, hi)):
+        summed[k].wait_recv()
+        out[:, side] = (inside[tops[k]] + reduced[k, :, side].astype(F32)).astype(BF16)
 
     for copy in relays + direct + summed:
         copy.wait_send()

time: 45 us -> 44.9 us (level)
  no operation moved by 1% of the time
where the time goes in v6:
time: 44.9 us; the launch traced here: 44.6 us
  Pallas kernels  43.9 us (98%)
  local copies, waits for them, and re-layouts  0.71 us (2%)
    pallas_call x1, Pallas kernels, local(): pl.pallas_call(functools.partial(kernel, groups), in_specs=[hbm] * 5 + [v...  43.9 us

profile of v6, /device:TPU:6, one launch (start us, length us, event | category | flops | bytes accessed | tf_op | source)
XLA Modules:
  0.0 44.6 jit_solution(4847288556382444815)
XLA Ops:
  0.0 43.9 %gated_delta_layer.1 = bf16[64,2048]{1,0:T(8,128)(2,1)S(1)} custom-call(bf16[256,2048]{1,0:T(8,128)(2,1)} %act.1, bf16[2048,512]{1,0:T(8,128)(2,1)} %w_q.1, bf16[2048,512]{1,0:T(8,128)(2,1)} %w_k.1, bf16[2048,1024]{1,0:T(8,128)(2,1)} %w_v.1, bf16[2048,1024]{1,0:T(8,128)(2,1)} %w_z.1, bf16[8,2048]{1,0:T(8,128)(2,1)} %bitcast.5, bf16[8,2048]{1,0:T(8,128)(2,1)} %bitcast.6, ...), custom_call_target="tpu_custom_call" | custom-call | tf_op jit(solution)/shard_map/gated_delta_layer/pallas_call | solution.py:482
  43.9 0.7 %copy.16 = bf16[64,2048]{1,0:T(8,128)(2,1)} copy(bf16[64,2048]{1,0:T(8,128)(2,1)S(1)} %gated_delta_layer.1) | data formatting | bytes 524288
